TPU v7x, 256 devices: a whole 4x4x8 slice. The times are simulated.
256 devices in a mesh: blk: 16 (over x_lo, y, core), rep: 16 (over x_hi, z).
Axes of the slice: x: 4 (x_hi: 2, x_lo: 2; x = x_hi * 2 + x_lo), y: 4, z: 8, core: 2. Of those that a mesh axis runs over, the one named last changes fastest.
Arguments:
- tokens: bfloat16 [196608, 576], P(('blk', 'rep')), may hold values from -6 to 6
- cotangent: bfloat16 [196608, 576], P(('blk', 'rep')), may hold values from -16 to 16
- gate_up: bfloat16 [16, 576, 1536], P('blk'), may hold values from -0.25 to 0.25
- down_proj: bfloat16 [16, 768, 576], P('blk'), may hold values from -0.21875 to 0.21875
- norm_gain: float32 [16, 576], P('blk'), may hold values from 0.1 to 1.9
Outputs:
- token_grad: bfloat16 [196608, 576], P(('blk', 'rep'))
- gate_up_grad: float32 [16, 576, 1536], P('blk', 'rep')
- down_grad: float32 [16, 768, 576], P('blk', None, 'rep')
- gain_grad: float32 [16, 576], P('blk', 'rep')
All inputs are finite; a program needn't handle non-finite values.
Results may differ from a plain program's by a relative error of at most 0.029.
Values may be sent and summed in bfloat16 or wider, within the bound.
No kernel may reach another device: no remote copies, remote signals or barrier semaphores. Data moves between devices by JAX's collectives and lax.ppermute only.
A program may use at most 128 MiB of HBM per device.

v0:
```python
import jax
import jax.numpy as jnp
from jax import lax
from jax.sharding import PartitionSpec as P

STEPS = 2


epsilon = 1e-05


def passed_along(x, axis, by):
    peers = lax.axis_size(axis)
    return lax.ppermute(x, axis, [(i, (i + by) % peers) for i in range(peers)])


def as_sent(x):

    def short(part):
        return part.astype(jnp.bfloat16) if part.dtype == jnp.float32 else part

    return jax.tree.map(short, x)


def norm_parts(hidden, norm_gain):
    floated = hidden.astype(jnp.float32)
    inverse = lax.rsqrt(jnp.mean(floated * floated, axis=-1, keepdims=True) + epsilon)
    normed = (floated * inverse * norm_gain).astype(jnp.bfloat16)
    return (floated, inverse, normed)


def layer_forward(hidden, gate_up, down_weight, norm_gain):
    floated, inverse, normed = norm_parts(hidden, norm_gain)
    projected = jnp.dot(normed, gate_up, preferred_element_type=jnp.float32)
    width = down_weight.shape[0]
    gate_part = projected[:, :width]
    up_part = projected[:, width:]
    activated = (gate_part * jax.nn.sigmoid(gate_part) * up_part).astype(jnp.bfloat16)
    return (floated + jnp.dot(activated, down_weight, preferred_element_type=jnp.float32)).astype(
        jnp.bfloat16
    )


def layer_backward(hidden, outgrad, gate_up, down_weight, norm_gain):
    floated, inverse, normed = norm_parts(hidden, norm_gain)
    projected = jnp.dot(normed, gate_up, preferred_element_type=jnp.float32)
    width = down_weight.shape[0]
    gate_part = projected[:, :width]
    up_part = projected[:, width:]
    sigmoid_part = jax.nn.sigmoid(gate_part)
    activated = (gate_part * sigmoid_part * up_part).astype(jnp.bfloat16)
    down_term = lax.dot_general(
        activated, outgrad, (((0,), (0,)), ((), ())), preferred_element_type=jnp.float32
    )
    act_grad = lax.dot_general(
        outgrad, down_weight, (((1,), (1,)), ((), ())), preferred_element_type=jnp.float32
    )
    gate_grad = act_grad * up_part * sigmoid_part * (1.0 + gate_part * (1.0 - sigmoid_part))
    up_grad = act_grad * gate_part * sigmoid_part
    mixed_grad = jnp.concatenate([gate_grad, up_grad], axis=1).astype(jnp.bfloat16)
    gate_up_term = lax.dot_general(
        normed, mixed_grad, (((0,), (0,)), ((), ())), preferred_element_type=jnp.float32
    )
    norm_grad = lax.dot_general(
        mixed_grad, gate_up, (((1,), (1,)), ((), ())), preferred_element_type=jnp.float32
    )
    gain_term = jnp.sum(norm_grad * floated * inverse, axis=0)
    scaled = norm_grad * norm_gain
    inner = jnp.mean(scaled * floated, axis=-1, keepdims=True)
    hidden_grad = (
        outgrad.astype(jnp.float32) + inverse * (scaled - floated * inverse * inverse * inner)
    ).astype(jnp.bfloat16)
    return (hidden_grad, gate_up_term, down_term, gain_term)


def per_device(tokens, cotangent, gate_up, down_proj, norm_gain):
    w_gate_up = gate_up[0]
    w_down = down_proj[0]
    w_gain = norm_gain[0]
    states = []
    kept = []
    hidden = tokens
    for cycle_step in range(STEPS):
        if cycle_step > 0:
            w_gate_up, w_down, w_gain = (
                passed_along(w_gate_up, "blk", -1),
                passed_along(w_down, "blk", -1),
                passed_along(w_gain.astype(jnp.bfloat16), "blk", -1).astype(w_gain.dtype),
            )
        kept.append((w_gate_up, w_down, w_gain))
        states.append(hidden)
        hidden = layer_forward(hidden, w_gate_up, w_down, w_gain)
    outgrad = cotangent
    carried = None
    for cycle_step in reversed(range(STEPS)):
        w_gate_up, w_down, w_gain = kept[cycle_step]
        outgrad, gu_term, down_term, gain_term = layer_backward(
            states[cycle_step], outgrad, w_gate_up, w_down, w_gain
        )
        if cycle_step < STEPS - 1:
            gu_prev, down_prev, gain_prev = jax.tree.map(
                lambda part, own: part.astype(own.dtype),
                passed_along(as_sent(carried), "blk", 1),
                carried,
            )
            carried = (gu_prev + gu_term, down_prev + down_term, gain_prev + gain_term)
        else:
            carried = (gu_term, down_term, gain_term)
    gu_final, down_final, gain_final = (
        lax.psum_scatter(
            carried[0].astype(jnp.bfloat16), "rep", scatter_dimension=0, tiled=True
        ).astype(jnp.float32),
        lax.psum_scatter(
            carried[1].astype(jnp.bfloat16), "rep", scatter_dimension=1, tiled=True
        ).astype(jnp.float32),
        lax.psum_scatter(
            carried[2].astype(jnp.bfloat16), "rep", scatter_dimension=0, tiled=True
        ).astype(jnp.float32),
    )
    return (outgrad, gu_final[None], down_final[None], gain_final[None])


def solution(mesh):
    placed = (
        P(("blk", "rep"), None),
        P(("blk", "rep"), None),
        P("blk", None, None),
        P("blk", None, None),
        P("blk", None),
    )
    return jax.shard_map(
        per_device,
        mesh=mesh,
        in_specs=placed,
        out_specs=(
            P(("blk", "rep"), None),
            P("blk", "rep", None),
            P("blk", None, "rep"),
            P("blk", "rep"),
        ),
        check_vma=False,
    )
```

profile of v0, /device:TPU:20, one launch (start us, length us, event | category | flops | bytes accessed | tf_op | source)
XLA Modules:
  0.0 177.0 jit_solution(279576429423773862)
XLA Ops:
  0.6 0.7 reduce
  1.3 0.1 collective-permute-start.1
  1.4 0.6 collective-permute-start
  2.0 0.1 collective-permute-start.2
  2.1 1.4 fusion.22
  3.5 3.9 %fusion.34 = f32[768,1536]{1,0:T(8,128)S(1)} fusion(bf16[768,576]{0,1:T(8,128)(2,1)} %param.5, f32[576]{0:T(1024)S(1)} %reduce, f32[768]{0:T(1024)S(1)} %add_rsqrt_fusion.1, bf16[1,576,1536]{2,1,0:T(8,128)(2,1)} %param.7), kind=kOutput, calls=%fused_computation.52 | convolution fusion | flops 1360723968 | bytes 7378176 | tf_op jit(solution)/shard_map/dot_general | solution.py:34
  7.4 0.0 copy-start
  7.4 0.0 copy-start.2
  7.4 0.0 copy-start.7
  7.4 0.7 multiply_convert_fusion.5
  8.1 1.5 copy-done
  9.6 0.0 copy-done.2
  9.6 0.6 copy-done.7
  10.1 0.0 copy-start.3
  10.1 0.0 copy-start.5
  10.1 0.9 fusion.18
  11.1 0.2 copy-done.3
  11.3 0.0 copy-done.5
  11.3 0.6 fusion.49
  13.1 0.0 collective-permute-done.1
  13.2 18.7 %collective-permute-done.2 = bf16[576,1536]{1,0:T(8,128)(2,1)} collective-permute-done((bf16[576,1536]{1,0:T(8,128)(2,1)}, bf16[576,1536]{1,0:T(8,128)(2,1)}, u32[]{:S(2)}, u32[]{:S(2)}) %collective-permute-start.2) | collective-permute-done | bytes 1769504 | tf_op jit(solution)/shard_map/ppermute | solution.py:14
  31.8 0.0 copy-start.4
  31.8 3.7 %fusion.31 = f32[768,1536]{1,0:T(8,128)S(1)} fusion(bf16[576,1536]{1,0:T(8,128)(2,1)} %collective-permute-done.2, bf16[768,576]{0,1:T(8,128)(2,1)S(1)} %get-tuple-element.27, f32[576]{0:T(1024)S(1)} %convert_element_type.81, f32[768]{0:T(1024)S(1)} %add_rsqrt_fusion), kind=kOutput, calls=%fused_computation.51 | convolution fusion | flops 1360723968 | bytes 7378176 | tf_op jit(solution)/shard_map/dot_general | solution.py:46
  35.5 0.0 copy-done.4
  35.5 1.9 %convolution_convert_fusion.1 = bf16[768,576]{0,1:T(8,128)(2,1)} fusion(bf16[768,576]{0,1:T(8,128)(2,1)S(1)} %copy-done.4, f32[768,1536]{1,0:T(8,128)S(1)} %fusion.31), kind=kOutput, calls=%fused_computation.50 | convolution fusion | flops 683458560 | bytes 6488064 | tf_op jit(solution)/shard_map/dot_general | solution.py:52
  37.4 0.0 collective-permute-done
  37.4 3.0 %multiply_convert_fusion.4 = (bf16[768,768]{1,0:T(8,128)(2,1)S(1)}, bf16[768,768]{1,0:T(8,128)(2,1)S(1)}) fusion(f32[768,1536]{1,0:T(8,128)S(1)} %fusion.31, bf16[768,576]{0,1:T(8,128)(2,1)S(1)} %copy-done.4, bf16[768,576]{0,1:T(8,128)(2,1)} %collective-permute-done), kind=kOutput, calls=%fused_computation.17 | convolution fusion | flops 687144960 | bytes 8847360 | tf_op jit(solution)/shard_map/dot_general | solution.py:55
  40.4 0.0 slice-start
  40.5 2.9 %convolution_convert_fusion = bf16[576,1536]{1,0:T(8,128)(2,1)} fusion(bf16[768,768]{1,0:T(8,128)(2,1)S(1)} %get-tuple-element.23, bf16[768,768]{1,0:T(8,128)(2,1)S(1)} %get-tuple-element.22, bf16[768,576]{0,1:T(8,128)(2,1)S(1)} %get-tuple-element.27, f32[576]{0:T(1024)S(1)} %convert_element_type.81, f32[768]{0:T(1024)S(1)} %add_rsqrt_fusion), kind=kOutput, calls=%fused_computation.10 | convolution fusion | flops 1366327296 | bytes 5018880 | tf_op jit(solution)/shard_map/dot_general | solution.py:61
  43.3 3.4 %fusion.21 = (bf16[576]{0:T(1024)(128)(2,1)S(1)}, f32[768]{0:T(1024)S(1)}, f32[768,576]{0,1:T(8,128)S(1)}) fusion(bf16[768,576]{0,1:T(8,128)(2,1)S(1)} %get-tuple-element.27, f32[768]{0:T(1024)S(1)} %add_rsqrt_fusion, f32[576]{0:T(1024)S(1)} %convert_element_type.81, bf16[576,1536]{1,0:T(8,128)(2,1)} %collective-permute-done.2, ...), kind=kOutput, calls=%fused_computation.40 | convolution fusion | flops 1366768384 | bytes 6792576 | tf_op jit(solution)/shard_map/dot_general | solution.py:64
  46.8 0.0 copy-start.8
  46.8 0.6 fusion.17
  47.4 0.0 slice-done
  47.4 0.0 slice-done.1
  47.4 0.5 copy-done.8
  47.9 2.0 %multiply_convert_fusion.2 = (bf16[768,768]{1,0:T(8,128)(2,1)S(1)}, bf16[768,768]{1,0:T(8,128)(2,1)S(1)}) fusion(f32[768,1536]{1,0:T(8,128)S(1)} %bitcast.45, bf16[768,576]{0,1:T(8,128)(2,1)S(1)} %fusion.17, bf16[1,768,576]{1,2,0:T(8,128)(2,1)S(1)} %copy-done.8), kind=kOutput, calls=%fused_computation.15 | convolution fusion | flops 687144960 | bytes 8847360 | tf_op jit(solution)/shard_map/dot_general | solution.py:55
  50.0 1.9 %collective-permute-start.5 = (bf16[576]{0:T(1024)(128)(2,1)S(1)}, bf16[576]{0:T(1024)(128)(2,1)S(1)}, u32[]{:S(2)}, u32[]{:S(2)}) collective-permute-start(bf16[576]{0:T(1024)(128)(2,1)S(1)} %get-tuple-element.12), channel_id=1, source_target_pairs={{0,16},{16,32},{32,48},{48,64},{64,80},{80,96},{96,112},{112,128},... | collective-permute-start | bytes 3464 | tf_op jit(solution)/shard_map/ppermute | solution.py:14
  51.9 0.1 collective-permute-start.4
  52.0 3.4 %collective-permute-start.3 = (bf16[576,1536]{1,0:T(8,128)(2,1)}, bf16[576,1536]{1,0:T(8,128)(2,1)S(1)}, u32[]{:S(2)}, u32[]{:S(2)}) collective-permute-start(bf16[576,1536]{1,0:T(8,128)(2,1)} %convolution_convert_fusion), channel_id=1, source_target_pairs={{0,16},{16,32},{32,48},{48,64},{64,80},{80,96},{96,112},{112,128},... | collective-permute-start | bytes 5308424 | tf_op jit(solution)/shard_map/ppermute | solution.py:14
  55.4 0.0 copy-done.6
  55.4 1.8 %fusion.26 = (f32[576]{0:T(1024)S(1)}, f32[768]{0:T(1024)S(1)}, f32[768,576]{0,1:T(8,128)S(1)}) fusion(bf16[768,576]{0,1:T(8,128)(2,1)S(1)} %copy-done.2, f32[768]{0:T(1024)S(1)} %add_rsqrt_fusion.1, f32[576]{0:T(1024)S(1)} %reduce, bf16[1,576,1536]{2,1,0:T(8,128)(2,1)S(1)} %copy-done.6, bf16[768,768]{1,0:T(8,128)(2,1)S(1)} %get-tuple-element.21, ...), kind=kOutput, calls=%fused_computation.45 | convolution fusion | flops 1366768384 | bytes 6793728 | tf_op jit(solution)/shard_map/dot_general | solution.py:64
  57.3 3.4 %fusion.27 = f32[576,1536]{1,0:T(8,128)} fusion(bf16[768,768]{1,0:T(8,128)(2,1)S(1)} %get-tuple-element.21, bf16[768,768]{1,0:T(8,128)(2,1)S(1)} %get-tuple-element.20, bf16[768,576]{0,1:T(8,128)(2,1)S(1)} %copy-done.2, f32[576]{0:T(1024)S(1)} %reduce, f32[768]{0:T(1024)S(1)} %add_rsqrt_fusion.1), kind=kOutput, calls=%fused_computation.47 | convolution fusion | flops 1365442560 | bytes 6788352 | tf_op jit(solution)/shard_map/dot_general | solution.py:61
  60.6 1.5 fusion.11
  62.1 0.0 collective-permute-done.5
  62.1 42.4 %all-reduce.2 = bf16[576]{0:T(1024)(128)(2,1)S(1)} all-reduce(bf16[576]{0:T(1024)(128)(2,1)S(1)} %add_convert_fusion.2), channel_id=4, replica_groups=mesh['blk'=16,'rep'=16] {'rep'}, use_global_device_ids=true, to_apply=%region_8.0.clone | all-reduce | flops 576 | bytes 2304
  104.6 0.0 collective-permute-done.4
  104.6 3.5 %add_convert_fusion.1 = bf16[768,576]{0,1:T(8,128)(2,1)} fusion(bf16[768,576]{0,1:T(8,128)(2,1)} %collective-permute-done.4, bf16[768,576]{0,1:T(8,128)(2,1)S(1)} %fusion.17, bf16[768,768]{1,0:T(8,128)(2,1)} %copy-done.3), kind=kOutput, calls=%fused_computation.46 | convolution fusion | flops 680804352 | bytes 3833856 | tf_op jit(solution)/shard_map/dot_general | solution.py:52
  108.0 0.0 collective-permute-done.3
  108.0 0.0 copy-done.1
  108.1 0.5 add_convert_fusion
  108.6 49.3 %fusion.48 = (bf16[40,1536]{1,0:T(8,128)(2,1)S(1)}, bf16[768,40]{0,1:T(8,128)(2,1)S(1)}) fusion(bf16[576,1536]{1,0:T(8,128)(2,1)S(1)} %add_convert_fusion, bf16[768,576]{0,1:T(8,128)(2,1)} %add_convert_fusion.1), kind=kCustom, calls=%all-reduce-scatter.2 | all-reduce-scatter fusion | flops 1474561 | bytes 2839552
  157.9 2.4 %collective-permute-start.8 = (bf16[768,40]{0,1:T(8,128)(2,1)S(1)}, bf16[768,40]{0,1:T(8,128)(2,1)S(1)}, u32[]{:S(2)}, u32[]{:S(2)}) collective-permute-start(bf16[768,40]{0,1:T(8,128)(2,1)S(1)} %get-tuple-element.19), channel_id=1, source_target_pairs={{0,1},{1,2},{2,3},{3,4},{4,5},{5,6},{6,7},{7,8},{8,9},{9,10},{10,1... | collective-permute-start | bytes 184328
  160.4 1.9 %collective-permute-start.9 = (bf16[768,20]{0,1:T(8,128)(2,1)S(1)}, bf16[768,20]{0,1:T(8,128)(2,1)S(1)}, u32[]{:S(2)}, u32[]{:S(2)}) collective-permute-start(bf16[768,20]{0,1:T(8,128)(2,1)S(1)} %slice.23), channel_id=1, source_target_pairs={{0,2},{1,3},{2,4},{3,5},{4,6},{5,7},{6,8},{7,9},{8,10},{9,11},{10,... | collective-permute-start | bytes 92168
  162.3 1.9 %collective-permute-start.6 = (bf16[40,1536]{1,0:T(8,128)(2,1)S(1)}, bf16[40,1536]{1,0:T(8,128)(2,1)S(1)}, u32[]{:S(2)}, u32[]{:S(2)}) collective-permute-start(bf16[40,1536]{1,0:T(8,128)(2,1)S(1)} %get-tuple-element.18), channel_id=1, source_target_pairs={{0,1},{1,2},{2,3},{3,4},{4,5},{5,6},{6,7},{7,8},{8,9},{9,10},{10,1... | collective-permute-start | bytes 368648
  164.2 0.6 bitcast_convert_fusion
  164.8 4.1 %collective-permute-start.7 = (bf16[20,1536]{1,0:T(8,128)(2,1)S(1)}, bf16[20,1536]{1,0:T(8,128)(2,1)S(1)}, u32[]{:S(2)}, u32[]{:S(2)}) collective-permute-start(bf16[20,1536]{1,0:T(8,128)(2,1)S(1)} %slice.22), channel_id=1, source_target_pairs={{0,2},{1,3},{2,4},{3,5},{4,6},{5,7},{6,8},{7,9},{8,10},{9,11},{10,... | collective-permute-start | bytes 184328
  169.0 1.7 collective-permute-done.9
  170.7 0.0 collective-permute-done.8
  170.7 0.3 concatenate.11
  171.1 0.8 copy.20
  171.9 3.8 %collective-permute-done.7 = bf16[20,1536]{1,0:T(8,128)(2,1)S(1)} collective-permute-done((bf16[20,1536]{1,0:T(8,128)(2,1)S(1)}, bf16[20,1536]{1,0:T(8,128)(2,1)S(1)}, u32[]{:S(2)}, u32[]{:S(2)}) %collective-permute-start.7) | collective-permute-done | bytes 61472
  175.7 0.0 collective-permute-done.6
  175.7 0.4 concatenate.10
  176.1 0.9 copy.19
  (15 shorter events, 0.1 us)
Async XLA Ops:
  1.3 11.8 %collective-permute-start.1 = (bf16[576]{0:T(1024)(128)(2,1)S(1)}, bf16[576]{0:T(1024)(128)(2,1)S(1)}, u32[]{:S(2)}, u32[]{:S(2)}) collective-permute-start(bf16[576]{0:T(1024)(128)(2,1)S(1)} %convert_element_type.80), channel_id=1, source_target_pairs={{0,240},{16,0},{32,16},{48,32},{64,48},{80,64},{96,80},{112,96},{1... | collective-permute-start | bytes 3464 | tf_op jit(solution)/shard_map/ppermute | solution.py:14
  1.4 36.0 %collective-permute-start = (bf16[768,576]{0,1:T(8,128)(2,1)}, bf16[768,576]{0,1:T(8,128)(2,1)}, u32[]{:S(2)}, u32[]{:S(2)}) collective-permute-start(bf16[768,576]{0,1:T(8,128)(2,1)} %bitcast.47), channel_id=1, source_target_pairs={{0,240},{16,0},{32,16},{48,32},{64,48},{80,64},{96,80},{112,96},{1... | collective-permute-start | bytes 2654216 | tf_op jit(solution)/shard_map/ppermute | solution.py:14
  2.0 29.8 %collective-permute-start.2 = (bf16[576,1536]{1,0:T(8,128)(2,1)}, bf16[576,1536]{1,0:T(8,128)(2,1)}, u32[]{:S(2)}, u32[]{:S(2)}) collective-permute-start(bf16[576,1536]{1,0:T(8,128)(2,1)} %bitcast.46), channel_id=1, source_target_pairs={{0,240},{16,0},{32,16},{48,32},{64,48},{80,64},{96,80},{112,96},{1... | collective-permute-start | bytes 5308424 | tf_op jit(solution)/shard_map/ppermute | solution.py:14
  7.4 2.2 %copy-start = (f32[768,1536]{1,0:T(8,128)}, f32[768,1536]{1,0:T(8,128)S(1)}, u32[]{:S(2)}) copy-start(f32[768,1536]{1,0:T(8,128)S(1)} %fusion.34) | copy-start | bytes 14155780
  7.4 2.2 %copy-start.2 = (bf16[768,576]{0,1:T(8,128)(2,1)S(1)}, bf16[768,576]{0,1:T(8,128)(2,1)}, u32[]{:S(2)}) copy-start(bf16[768,576]{0,1:T(8,128)(2,1)} %param.5) | copy-start | bytes 2654212
  7.4 2.8 %copy-start.7 = (bf16[1,768,576]{1,2,0:T(8,128)(2,1)S(1)}, bf16[1,768,576]{1,2,0:T(8,128)(2,1)}, u32[]{:S(2)}) copy-start(bf16[1,768,576]{1,2,0:T(8,128)(2,1)} %param.8) | copy-start | bytes 2654212
  10.1 1.1 copy-start.3
  10.1 1.1 copy-start.5
  31.8 3.7 %copy-start.4 = (bf16[768,576]{0,1:T(8,128)(2,1)S(1)}, bf16[768,576]{0,1:T(8,128)(2,1)}, u32[]{:S(2)}) copy-start(bf16[768,576]{0,1:T(8,128)(2,1)} %param.6) | copy-start | bytes 2654212
  40.4 6.9 %slice-start = ((s8[4718592]{0:T(1024)(128)(4,1)}), s8[524288]{0:T(1024)(128)(4,1)S(1)}, s32[]{:S(2)}) async-start(s8[4718592]{0:T(1024)(128)(4,1)} %bitcast.44), calls=%async_computation | async-start | bytes 1048576
  43.3 4.1 %slice-start.1 = ((s8[4718592]{0:T(1024)(128)(4,1)}), s8[4194304]{0:T(1024)(128)(4,1)S(1)}, s32[]{:S(2)}) async-start(s8[4718592]{0:T(1024)(128)(4,1)} %bitcast.44), calls=%async_computation.1 | async-start | bytes 8388608
  46.8 1.2 copy-start.8
  47.9 7.5 %copy-start.6 = (bf16[1,576,1536]{2,1,0:T(8,128)(2,1)S(1)}, bf16[1,576,1536]{2,1,0:T(8,128)(2,1)}, u32[]{:S(2)}) copy-start(bf16[1,576,1536]{2,1,0:T(8,128)(2,1)} %param.7) | copy-start | bytes 5308420
  50.0 12.1 %collective-permute-start.5 = (bf16[576]{0:T(1024)(128)(2,1)S(1)}, bf16[576]{0:T(1024)(128)(2,1)S(1)}, u32[]{:S(2)}, u32[]{:S(2)}) collective-permute-start(bf16[576]{0:T(1024)(128)(2,1)S(1)} %get-tuple-element.12), channel_id=1, source_target_pairs={{0,16},{16,32},{32,48},{48,64},{64,80},{80,96},{96,112},{112,128},... | collective-permute-start | bytes 3464 | tf_op jit(solution)/shard_map/ppermute | solution.py:14
  51.9 52.7 %collective-permute-start.4 = (bf16[768,576]{0,1:T(8,128)(2,1)}, bf16[768,576]{0,1:T(8,128)(2,1)}, u32[]{:S(2)}, u32[]{:S(2)}) collective-permute-start(bf16[768,576]{0,1:T(8,128)(2,1)} %convolution_convert_fusion.1), channel_id=1, source_target_pairs={{0,16},{16,32},{32,48},{48,64},{64,80},{80,96},{96,112},{112,128},... | collective-permute-start | bytes 2654216 | tf_op jit(solution)/shard_map/ppermute | solution.py:14
  52.0 56.0 %collective-permute-start.3 = (bf16[576,1536]{1,0:T(8,128)(2,1)}, bf16[576,1536]{1,0:T(8,128)(2,1)S(1)}, u32[]{:S(2)}, u32[]{:S(2)}) collective-permute-start(bf16[576,1536]{1,0:T(8,128)(2,1)} %convolution_convert_fusion), channel_id=1, source_target_pairs={{0,16},{16,32},{32,48},{48,64},{64,80},{80,96},{96,112},{112,128},... | collective-permute-start | bytes 5308424 | tf_op jit(solution)/shard_map/ppermute | solution.py:14
  104.6 3.5 %copy-start.1 = (f32[576,1536]{1,0:T(8,128)S(1)}, f32[576,1536]{1,0:T(8,128)}, u32[]{:S(2)}) copy-start(f32[576,1536]{1,0:T(8,128)} %fusion.27) | copy-start | bytes 10616836
  157.9 12.8 %collective-permute-start.8 = (bf16[768,40]{0,1:T(8,128)(2,1)S(1)}, bf16[768,40]{0,1:T(8,128)(2,1)S(1)}, u32[]{:S(2)}, u32[]{:S(2)}) collective-permute-start(bf16[768,40]{0,1:T(8,128)(2,1)S(1)} %get-tuple-element.19), channel_id=1, source_target_pairs={{0,1},{1,2},{2,3},{3,4},{4,5},{5,6},{6,7},{7,8},{8,9},{9,10},{10,1... | collective-permute-start | bytes 184328
  160.4 10.4 %collective-permute-start.9 = (bf16[768,20]{0,1:T(8,128)(2,1)S(1)}, bf16[768,20]{0,1:T(8,128)(2,1)S(1)}, u32[]{:S(2)}, u32[]{:S(2)}) collective-permute-start(bf16[768,20]{0,1:T(8,128)(2,1)S(1)} %slice.23), channel_id=1, source_target_pairs={{0,2},{1,3},{2,4},{3,5},{4,6},{5,7},{6,8},{7,9},{8,10},{9,11},{10,... | collective-permute-start | bytes 92168
  162.3 13.4 %collective-permute-start.6 = (bf16[40,1536]{1,0:T(8,128)(2,1)S(1)}, bf16[40,1536]{1,0:T(8,128)(2,1)S(1)}, u32[]{:S(2)}, u32[]{:S(2)}) collective-permute-start(bf16[40,1536]{1,0:T(8,128)(2,1)S(1)} %get-tuple-element.18), channel_id=1, source_target_pairs={{0,1},{1,2},{2,3},{3,4},{4,5},{5,6},{6,7},{7,8},{8,9},{9,10},{10,1... | collective-permute-start | bytes 368648
  164.8 10.8 %collective-permute-start.7 = (bf16[20,1536]{1,0:T(8,128)(2,1)S(1)}, bf16[20,1536]{1,0:T(8,128)(2,1)S(1)}, u32[]{:S(2)}, u32[]{:S(2)}) collective-permute-start(bf16[20,1536]{1,0:T(8,128)(2,1)S(1)} %slice.22), channel_id=1, source_target_pairs={{0,2},{1,3},{2,4},{3,5},{4,6},{5,7},{6,8},{7,9},{8,10},{9,11},{10,... | collective-permute-start | bytes 184328
where the time goes:
time: 179 us; the launch traced here: 177 us
  blocking collectives  91.8 us (51%)
  matrix products  30.4 us (17%)
  waiting for transfers between devices  24.2 us (14%)
  starting transfers between devices  16.6 us (9%)
  other arithmetic  6.09 us (3%)
  local copies, waits for them, and re-layouts  5.81 us (3%)
  between operations  2.19 us (1%)
    unnamed x2, blocking collectives  91.8 us
    ppermute x6, waiting for transfers between devices, passed_along(): return lax.ppermute(x, axis, [(i, (i + by) % peers) for i in range(peers)])  18.7 us
    unnamed x4, starting transfers between devices  10.4 us
    dot_general x2, matrix products, layer_backward(): lax.dot_general(normed, mixed_grad, (((0,), (0,)), ((), ())), preferred_e...  6.21 us
    ppermute x6, starting transfers between devices, passed_along(): return lax.ppermute(x, axis, [(i, (i + by) % peers) for i in range(peers)])  6.17 us
    unnamed x29, local copies, waits for them, and re-layouts  5.81 us
    unnamed x4, waiting for transfers between devices  5.53 us
    dot_general x2, matrix products, layer_backward(): lax.dot_general(activated, outgrad, (((0,), (0,)), ((), ())), preferred_e...  5.38 us
  transfers between devices with their start and end apart: 10, of which 3 were waited for; matrix products, arithmetic and copies ran while one was open for 14% of the time, Pallas kernels for 0%

commit v1 on v0

v1 whole, which is shorter than its diff:
```python
import functools

import jax
import jax.numpy as jnp
from jax import lax
from jax.experimental import pallas as pl
from jax.experimental.pallas import tpu as pltpu
from jax.sharding import PartitionSpec as P

CHUNKS = 2

epsilon = 1e-05
bf16 = jnp.bfloat16
f32 = jnp.float32


def dot(a, b, contract):
    return lax.dot_general(a, b, ((contract[0], contract[1]), ((), ())), preferred_element_type=f32)


def norm_parts(hidden, gain):
    floated = hidden.astype(f32)
    inverse = lax.rsqrt(jnp.mean(floated * floated, axis=-1, keepdims=True) + epsilon)
    return floated, inverse, (floated * inverse * gain).astype(bf16)


def project(normed, gate_up):
    projected = dot(normed, gate_up, ((1,), (0,)))
    width = gate_up.shape[1] // 2
    gate_part = projected[:, :width]
    up_part = projected[:, width:]
    sig = jax.nn.sigmoid(gate_part)
    silu = gate_part * sig
    slope = up_part * sig * (1.0 + gate_part * (1.0 - sig))
    return (silu * up_part).astype(bf16), slope, silu


def back_through_norm(norm_grad, floated, inverse, outgrad, gain):
    gain_term = jnp.sum(norm_grad * floated * inverse, axis=0, keepdims=True)
    scaled = norm_grad * gain
    inner = jnp.mean(scaled * floated, axis=-1, keepdims=True)
    in_grad = outgrad.astype(f32) + inverse * (scaled - floated * (inverse * inverse * inner))
    return in_grad.astype(bf16), gain_term


def forward_kernel(h_ref, gu_ref, dn_ref, gain_ref, next_ref, normed_ref, act_ref, slope_ref, silu_ref):
    floated, _, normed = norm_parts(h_ref[...], gain_ref[...])
    normed_ref[...] = normed
    activated, slope, silu = project(normed, gu_ref[...])
    act_ref[...] = activated
    slope_ref[...] = slope.astype(bf16)
    silu_ref[...] = silu.astype(bf16)
    next_ref[...] = (floated + dot(activated, dn_ref[...], ((1,), (0,)))).astype(bf16)


def turn_kernel(h_ref, out_ref, gu_ref, dn_ref, gain_ref, in_ref, normed_ref, act_ref, mixed_ref, gain_term_ref):
    floated, inverse, normed = norm_parts(h_ref[...], gain_ref[...])
    normed_ref[...] = normed
    activated, slope, silu = project(normed, gu_ref[...])
    act_ref[...] = activated
    act_grad = dot(out_ref[...], dn_ref[...], ((1,), (1,)))
    mixed = jnp.concatenate([(act_grad * slope).astype(bf16), (act_grad * silu).astype(bf16)], axis=1)
    mixed_ref[...] = mixed
    norm_grad = dot(mixed, gu_ref[...], ((1,), (1,)))
    in_ref[...], gain_term_ref[...] = back_through_norm(norm_grad, floated, inverse, out_ref[...], gain_ref[...])


def backward_kernel(h_ref, out_ref, slope_ref, silu_ref, gu_ref, dn_ref, gain_ref, in_ref, mixed_ref, gain_term_ref):
    act_grad = dot(out_ref[...], dn_ref[...], ((1,), (1,)))
    mixed = jnp.concatenate(
        [
            (act_grad * slope_ref[...].astype(f32)).astype(bf16),
            (act_grad * silu_ref[...].astype(f32)).astype(bf16),
        ],
        axis=1,
    )
    mixed_ref[...] = mixed
    norm_grad = dot(mixed, gu_ref[...], ((1,), (1,)))
    floated, inverse, _ = norm_parts(h_ref[...], gain_ref[...])
    in_ref[...], gain_term_ref[...] = back_through_norm(norm_grad, floated, inverse, out_ref[...], gain_ref[...])


def weight_kernel(count, *refs):
    lefts, rights, total_ref = refs[:count], refs[count : 2 * count], refs[2 * count]
    total = None
    for left, right in zip(lefts, rights):
        term = dot(left[...], right[...], ((0,), (0,)))
        total = term if total is None else total + term
    total_ref[...] = total.astype(bf16)


def call(kernel, outs, args, flops):
    moved = sum(a.size * a.dtype.itemsize for a in args) + sum(s.size * s.dtype.itemsize for s in outs)
    return pl.pallas_call(
        kernel,
        out_shape=outs,
        compiler_params=pltpu.CompilerParams(vmem_limit_bytes=56 * 2**20),
        cost_estimate=pl.CostEstimate(flops=flops, bytes_accessed=moved, transcendentals=0),
    )(*args)


def passed_along(x, axis, by):
    peers = lax.axis_size(axis)
    return lax.ppermute(x, axis, [(i, (i + by) % peers) for i in range(peers)])


def per_device(tokens, cotangent, gate_up, down_proj, norm_gain):
    gate_up, down, gain = gate_up[0], down_proj[0], norm_gain
    rows, width = tokens.shape
    hid = down.shape[0]
    size = rows // CHUNKS
    wide = lambda n, dtype=bf16: jax.ShapeDtypeStruct((size, n), dtype)
    row = jax.ShapeDtypeStruct((1, width), f32)
    unit = 2 * size * width * hid
    parts = [slice(i * size, (i + 1) * size) for i in range(CHUNKS)]
    first, sent, cots = [], [], []
    for part in parts:
        cots.append(passed_along(cotangent[part], "blk", 1))
        nxt, *kept = call(
            forward_kernel,
            [wide(width), wide(width), wide(hid), wide(hid), wide(hid)],
            (tokens[part], gate_up, down, gain),
            3 * unit,
        )
        first.append(kept)
        sent.append(passed_along(nxt, "blk", 1))
    turned, returned = [], []
    for hidden, cot in zip(sent, cots):
        in_grad, *kept = call(
            turn_kernel,
            [wide(width), wide(width), wide(hid), wide(2 * hid), row],
            (hidden, cot, gate_up, down, gain),
            5 * unit,
        )
        turned.append(kept)
        returned.append(passed_along(in_grad, "blk", -1))
    token_grads, mixed, gain_terms = [], [], [kept[3] for kept in turned]
    for part, out, kept in zip(parts, returned, first):
        token_grad, mixed_grad, gain_term = call(
            backward_kernel,
            [wide(width), wide(2 * hid), row],
            (tokens[part], out, kept[2], kept[3], gate_up, down, gain),
            3 * unit,
        )
        token_grads.append(token_grad)
        mixed.append(mixed_grad)
        gain_terms.append(gain_term)
    weight = functools.partial(weight_kernel, 2 * CHUNKS)
    (down_term,) = call(
        weight,
        [jax.ShapeDtypeStruct((width, hid), bf16)],
        (*cots, *returned, *[kept[1] for kept in turned], *[kept[1] for kept in first]),
        2 * CHUNKS * unit,
    )
    (gate_up_term,) = call(
        weight,
        [jax.ShapeDtypeStruct((width, 2 * hid), bf16)],
        (*[kept[0] for kept in turned], *[kept[0] for kept in first], *[kept[2] for kept in turned], *mixed),
        4 * CHUNKS * unit,
    )
    gain_sum = functools.reduce(jnp.add, gain_terms).astype(bf16)
    tail = jnp.pad(gain_sum, ((0, 15), (0, 2 * hid - width)))
    gate_up_term = jnp.concatenate([gate_up_term, tail], axis=0)
    gate_up_all, down_all = lax.psum((gate_up_term, down_term), "rep")
    share = width // lax.axis_size("rep")
    start = lax.axis_index("rep") * share
    gate_up_mine = lax.dynamic_slice_in_dim(gate_up_all, start, share, 0).astype(f32)
    down_mine = lax.dynamic_slice_in_dim(down_all, start, share, 0).astype(f32).T
    gain_mine = lax.dynamic_slice_in_dim(gate_up_all[width], start, share, 0).astype(f32)
    return jnp.concatenate(token_grads, axis=0), gate_up_mine[None], down_mine[None], gain_mine[None]


def solution(mesh):
    placed = (
        P(("blk", "rep"), None),
        P(("blk", "rep"), None),
        P("blk", None, None),
        P("blk", None, None),
        P("blk", None),
    )
    return jax.shard_map(
        per_device,
        mesh=mesh,
        in_specs=placed,
        out_specs=(
            P(("blk", "rep"), None),
            P("blk", "rep", None),
            P("blk", None, "rep"),
            P("blk", "rep"),
        ),
        check_vma=False,
    )
```

time: 179 us -> 260 us (1.45)
  waiting for transfers between devices: 24.2 us -> 176 us
  blocking collectives: 91.8 us -> 0 us
  Pallas kernels: 0 us -> 45.4 us
  matrix products: 30.4 us -> 0 us
  starting transfers between devices: 16.6 us -> 2.56 us
  between operations: 2.19 us -> 14.1 us
  local copies, waits for them, and re-layouts: 5.81 us -> 13 us
    psum x0 -> x1, waiting for transfers between devices: none -> 166 us  [per_device(): gate_up_all, down_all = lax.psum((gate_up_term, down_term), 'rep')]
    unnamed x2 -> x0, blocking collectives: 91.8 us -> none
    pallas_call x0 -> x8, Pallas kernels: none -> 45.4 us  [call(): pl.pallas_call(kernel, out_shape=outs, compiler_params=pltpu.CompilerPara...]
    dot_general x11 -> x0, matrix products: 30.4 us -> none  [the longest x2 6.21 us: layer_backward(): lax.dot_general(normed, mixed_grad, (((0,), (0,)), ((), ())), preferred_e...]
    unnamed x4 -> x0, starting transfers between devices: 10.4 us -> none
    ppermute x6, waiting for transfers between devices: 18.7 us -> 9.1 us  [passed_along(): return lax.ppermute(x, axis, [(i, (i + by) % peers) for i in range(peers)])]
    unnamed x29 -> x32, local copies, waits for them, and re-layouts: 5.81 us -> 12.1 us
    unnamed x4 -> x1, waiting for transfers between devices: 5.53 us -> 0.02 us
  transfers between devices with their start and end apart: 10 -> 7, of which waited for: 3 -> 4; matrix products, arithmetic and copies ran while one was open for 14% -> 1% of each run, Pallas kernels for 0% -> 9%
where the time goes in v1:
time: 260 us; the launch traced here: 257 us
  waiting for transfers between devices  176 us (68%)
  Pallas kernels  45.4 us (17%)
  between operations  14.1 us (5%)
  local copies, waits for them, and re-layouts  13 us (5%)
  other arithmetic  6.05 us (2%)
    psum x1, waiting for transfers between devices, per_device(): gate_up_all, down_all = lax.psum((gate_up_term, down_term), 'rep')  166 us
    pallas_call x8, Pallas kernels, call(): pl.pallas_call(kernel, out_shape=outs, compiler_params=pltpu.CompilerPara...  45.4 us
    unnamed x32, local copies, waits for them, and re-layouts  12.1 us
    ppermute x6, waiting for transfers between devices, passed_along(): return lax.ppermute(x, axis, [(i, (i + by) % peers) for i in range(peers)])  9.1 us
  transfers between devices with their start and end apart: 7, of which 4 were waited for; matrix products, arithmetic and copies ran while one was open for 1% of the time, Pallas kernels for 9%

profile of v1, /device:TPU:20, one launch (start us, length us, event | category | flops | bytes accessed | tf_op | source)
XLA Modules:
  0.0 256.7 jit_solution(17376647038899472635)
XLA Ops:
  7.2 0.0 copy-start.2
  7.2 0.0 all-reduce.4.cloned.1.call-start
  7.2 2.3 copy.10
  9.5 0.0 copy-done.2
  9.5 0.1 fusion.4
  9.6 1.0 copy.17.h_ref
  10.6 0.0 copy-start.3
  10.6 4.6 %shard_map.84 = (bf16[384,576]{1,0:T(8,128)(2,1)}, bf16[384,576]{1,0:T(8,128)(2,1)}, bf16[384,768]{1,0:T(8,128)(2,1)}, bf16[384,768]{1,0:T(8,128)(2,1)}, bf16[384,768]{1,0:T(8,128)(2,1)}) custom-call(bf16[384,576]{1,0:T(8,128)(2,1)} %copy.17.h_ref, bf16[576,1536]{1,0:T(8,128)(2,1)} %bitcast.15, bf16[768,576]{1,0:T(8,128)(2,1)} %bitcast.9, f32[1,576]{1,0:T(1,128)} %gain_ref.11), custom_call_target="tpu_custom_call" | custom-call | flops 1019215872 | bytes 5753088 | tf_op jit(solution)/shard_map/pallas_call | solution.py:94
  15.3 0.0 collective-permute-start
  15.3 0.0 copy-done.3
  15.3 0.1 fusion.3
  15.4 0.3 copy.18
  15.7 1.5 collective-permute-start.1
  17.1 1.0 copy.19.h_ref
  18.1 4.6 %shard_map.87 = (bf16[384,576]{1,0:T(8,128)(2,1)}, bf16[384,576]{1,0:T(8,128)(2,1)}, bf16[384,768]{1,0:T(8,128)(2,1)}, bf16[384,768]{1,0:T(8,128)(2,1)}, bf16[384,768]{1,0:T(8,128)(2,1)}) custom-call(bf16[384,576]{1,0:T(8,128)(2,1)} %copy.19.h_ref, bf16[576,1536]{1,0:T(8,128)(2,1)} %bitcast.16, bf16[768,576]{1,0:T(8,128)(2,1)} %bitcast.10, f32[1,576]{1,0:T(1,128)} %gain_ref.11), custom_call_target="tpu_custom_call" | custom-call | flops 1019215872 | bytes 5753088 | tf_op jit(solution)/shard_map/pallas_call | solution.py:94
  22.7 0.0 collective-permute-start.3
  22.7 0.3 copy.20
  23.0 1.0 collective-permute-start.4
  24.0 0.0 collective-permute-done.h_ref
  24.0 0.0 copy-start.11
  24.0 5.0 %collective-permute-done.1.out_ref.refs_0_ = bf16[384,576]{1,0:T(8,128)(2,1)S(1)} collective-permute-done((bf16[384,576]{1,0:T(8,128)(2,1)S(1)}, bf16[384,576]{1,0:T(8,128)(2,1)S(1)}, u32[]{:S(2)}, u32[]{:S(2)}) %collective-permute-start.1) | collective-permute-done | bytes 442400 | tf_op jit(solution)/shard_map/ppermute | solution.py:104
  29.0 0.0 copy-done.11
  29.0 0.0 copy-start.4
  29.0 0.8 copy-done.4
  29.8 6.2 %shard_map.85 = (bf16[384,576]{1,0:T(8,128)(2,1)}, bf16[384,576]{1,0:T(8,128)(2,1)}, bf16[384,768]{1,0:T(8,128)(2,1)}, bf16[384,1536]{1,0:T(8,128)(2,1)}, f32[1,576]{1,0:T(1,128)}) custom-call(bf16[384,576]{1,0:T(8,128)(2,1)} %copy-done.11, bf16[384,576]{1,0:T(8,128)(2,1)} %copy-done.4, bf16[576,1536]{1,0:T(8,128)(2,1)} %bitcast.17, ...), custom_call_target="tpu_custom_call" | custom-call | flops 1698693120 | bytes 6197760 | tf_op jit(solution)/shard_map/pallas_call | solution.py:94
  36.0 0.0 collective-permute-start.2
  36.0 0.0 collective-permute-done.3.h_ref
  36.0 3.6 %collective-permute-done.4.out_ref.refs_1_ = bf16[384,576]{1,0:T(8,128)(2,1)S(1)} collective-permute-done((bf16[384,576]{1,0:T(8,128)(2,1)S(1)}, bf16[384,576]{1,0:T(8,128)(2,1)S(1)}, u32[]{:S(2)}, u32[]{:S(2)}) %collective-permute-start.4) | collective-permute-done | bytes 442400 | tf_op jit(solution)/shard_map/ppermute | solution.py:104
  39.6 0.0 copy-start.5
  39.6 0.8 copy-done.5
  40.4 6.2 %shard_map.88 = (bf16[384,576]{1,0:T(8,128)(2,1)}, bf16[384,576]{1,0:T(8,128)(2,1)}, bf16[384,768]{1,0:T(8,128)(2,1)}, bf16[384,1536]{1,0:T(8,128)(2,1)}, f32[1,576]{1,0:T(1,128)}) custom-call(bf16[384,576]{1,0:T(8,128)(2,1)} %collective-permute-done.3.h_ref, bf16[384,576]{1,0:T(8,128)(2,1)} %copy-done.5, bf16[576,1536]{1,0:T(8,128)(2,1)} %bitcast.18, ...), custom_call_target="tpu_custom_call" | custom-call | flops 1698693120 | bytes 6197760 | tf_op jit(solution)/shard_map/pallas_call | solution.py:94
  46.5 0.0 collective-permute-start.5
  46.5 0.0 collective-permute-done.2.out_ref.refs_2_
  46.5 0.0 copy-start
  46.5 0.8 copy-done
  47.3 5.3 %shard_map.86 = (bf16[384,576]{1,0:T(8,128)(2,1)}, bf16[384,1536]{1,0:T(8,128)(2,1)}, f32[1,576]{1,0:T(1,128)}) custom-call(bf16[384,576]{1,0:T(8,128)(2,1)} %copy.17.h_ref, bf16[384,576]{1,0:T(8,128)(2,1)} %copy-done, bf16[384,768]{1,0:T(8,128)(2,1)} %get-tuple-element.32.slope_ref, bf16[384,768]{1,0:T(8,128)(2,1)} %get-tuple-element.33.silu_ref, ...), custom_call_target="tpu_custom_call" | custom-call | flops 1019215872 | bytes 6345216 | tf_op jit(solution)/shard_map/pallas_call | solution.py:94
  52.7 0.5 collective-permute-done.5.out_ref.refs_3_
  53.2 0.0 copy-start.1
  53.2 0.8 copy-done.1
  54.0 0.0 copy-start.8
  54.0 0.0 copy-start.9
  54.0 0.0 copy-start.10
  54.0 5.4 %shard_map.89 = (bf16[384,576]{1,0:T(8,128)(2,1)}, bf16[384,1536]{1,0:T(8,128)(2,1)}, f32[1,576]{1,0:T(1,128)}) custom-call(bf16[384,576]{1,0:T(8,128)(2,1)} %copy.19.h_ref, bf16[384,576]{1,0:T(8,128)(2,1)} %copy-done.1, bf16[384,768]{1,0:T(8,128)(2,1)} %get-tuple-element.37.slope_ref, bf16[384,768]{1,0:T(8,128)(2,1)} %get-tuple-element.38.silu_ref, ...), custom_call_target="tpu_custom_call" | custom-call | flops 1019215872 | bytes 6345216 | tf_op jit(solution)/shard_map/pallas_call | solution.py:94
  59.3 0.0 copy-done.8
  59.3 0.0 copy-done.9
  59.3 0.0 copy-done.10
  59.3 0.7 add_convert_fusion
  60.0 8.0 %shard_map.90 = bf16[576,1536]{1,0:T(8,128)(2,1)} custom-call(bf16[384,576]{1,0:T(8,128)(2,1)} %get-tuple-element.40.refs_0_, bf16[384,576]{1,0:T(8,128)(2,1)} %get-tuple-element.41.refs_1_, bf16[384,576]{1,0:T(8,128)(2,1)} %get-tuple-element.42.refs_2_, bf16[384,576]{1,0:T(8,128)(2,1)} %get-tuple-element.43.refs_3_, ...), custom_call_target="tpu_custom_call" | custom-call | flops 2717908992 | bytes 8257536 | tf_op jit(solution)/shard_map/pallas_call | solution.py:94
  68.0 2.8 %fusion.1 = bf16[592,1536]{1,0:T(8,128)(2,1)} fusion(bf16[1,576]{1,0:T(2,128)(2,1)S(1)} %add_convert_fusion, bf16[576,1536]{1,0:T(8,128)(2,1)} %shard_map.90), kind=kLoop, calls=%fused_computation.2 | loop fusion | flops 5455872 | bytes 3589248 | tf_op jit(solution)/shard_map/concatenate | solution.py:163
  70.9 5.2 %shard_map.91 = bf16[576,768]{1,0:T(8,128)(2,1)} custom-call(bf16[384,576]{1,0:T(8,128)(2,1)} %copy-done.4, bf16[384,576]{1,0:T(8,128)(2,1)} %copy-done.5, bf16[384,576]{1,0:T(8,128)(2,1)} %copy-done, bf16[384,576]{1,0:T(8,128)(2,1)} %copy-done.1, bf16[384,768]{1,0:T(8,128)(2,1)} %get-tuple-element.52.refs_4_, bf16[384,768]{1,0:T(8,128)(2,1)} %get-tuple-element.53.refs_5_, ...), custom_call_target="tpu_custom_call" | custom-call | flops 1358954496 | bytes 5013504 | tf_op jit(solution)/shard_map/pallas_call | solution.py:94
  76.0 0.0 copy-start.6
  76.0 0.0 copy-start.7
  76.0 0.0 all-reduce.4.cloned.1.call-update
  76.1 1.0 copy-done.6
  77.1 0.1 copy-done.7
  77.2 0.1 pad_maximum_fusion
  77.3 1.3 copy.14
  78.6 166.5 %all-reduce.4.cloned.1.call-done = (bf16[592,1536]{1,0:T(8,128)(2,1)}, bf16[576,768]{1,0:T(8,128)(2,1)}) async-done(((bf16[592,1536]{1,0:T(8,128)(2,1)}, bf16[576,768]{1,0:T(8,128)(2,1)}), (bf16[592,1536]{1,0:T(8,128)(2,1)}, bf16[576,768]{1,0:T(8,128)(2,1)})) %all-reduce.4.cloned.1.call-update) | async-done | bytes 2703376 | tf_op jit(solution)/shard_map/psum | solution.py:164
  245.1 0.7 slice.22
  245.8 0.9 bitcast_convert_fusion
  246.7 0.9 copy.15
  247.7 0.9 convert_bitcast_fusion
  248.6 0.8 copy.16
  249.3 0.6 fusion.2
Async XLA Ops:
  7.2 2.4 copy-start.2
  7.2 237.9 %all-reduce.4.cloned.1.call-start = ((), (), s32[]{:S(2)}) async-start(), calls=%async_computation | async-start | bytes 5406720 | tf_op jit(solution)/shard_map/psum | solution.py:164
  10.6 4.7 %copy-start.3 = (bf16[768,576]{0,1:T(8,128)(2,1)S(1)}, bf16[768,576]{0,1:T(8,128)(2,1)}, u32[]{:S(2)}) copy-start(bf16[768,576]{0,1:T(8,128)(2,1)} %param.6) | copy-start | bytes 2654212
  15.3 8.7 %collective-permute-start = (bf16[384,576]{1,0:T(8,128)(2,1)}, bf16[384,576]{1,0:T(8,128)(2,1)S(1)}, u32[]{:S(2)}, u32[]{:S(2)}) collective-permute-start(bf16[384,576]{1,0:T(8,128)(2,1)} %get-tuple-element.30), channel_id=1, source_target_pairs={{0,16},{16,32},{32,48},{48,64},{64,80},{80,96},{96,112},{112,128},... | collective-permute-start | bytes 1327112 | tf_op jit(solution)/shard_map/ppermute | solution.py:104
  15.7 13.4 %collective-permute-start.1 = (bf16[384,576]{1,0:T(8,128)(2,1)S(1)}, bf16[384,576]{1,0:T(8,128)(2,1)S(1)}, u32[]{:S(2)}, u32[]{:S(2)}) collective-permute-start(bf16[384,576]{1,0:T(8,128)(2,1)S(1)} %copy.18), channel_id=1, source_target_pairs={{0,16},{16,32},{32,48},{48,64},{64,80},{80,96},{96,112},{112,128},... | collective-permute-start | bytes 1327112 | tf_op jit(solution)/shard_map/ppermute | solution.py:104
  22.7 13.3 %collective-permute-start.3 = (bf16[384,576]{1,0:T(8,128)(2,1)}, bf16[384,576]{1,0:T(8,128)(2,1)}, u32[]{:S(2)}, u32[]{:S(2)}) collective-permute-start(bf16[384,576]{1,0:T(8,128)(2,1)} %get-tuple-element.35), channel_id=1, source_target_pairs={{0,16},{16,32},{32,48},{48,64},{64,80},{80,96},{96,112},{112,128},... | collective-permute-start | bytes 1327112 | tf_op jit(solution)/shard_map/ppermute | solution.py:104
  23.0 16.6 %collective-permute-start.4 = (bf16[384,576]{1,0:T(8,128)(2,1)S(1)}, bf16[384,576]{1,0:T(8,128)(2,1)S(1)}, u32[]{:S(2)}, u32[]{:S(2)}) collective-permute-start(bf16[384,576]{1,0:T(8,128)(2,1)S(1)} %copy.20), channel_id=1, source_target_pairs={{0,16},{16,32},{32,48},{48,64},{64,80},{80,96},{96,112},{112,128},... | collective-permute-start | bytes 1327112 | tf_op jit(solution)/shard_map/ppermute | solution.py:104
  24.0 5.0 %copy-start.11 = (bf16[384,576]{1,0:T(8,128)(2,1)}, bf16[384,576]{1,0:T(8,128)(2,1)S(1)}, u32[]{:S(2)}) copy-start(bf16[384,576]{1,0:T(8,128)(2,1)S(1)} %collective-permute-done.h_ref) | copy-start | bytes 1327108
  29.0 0.8 copy-start.4
  36.0 10.5 %collective-permute-start.2 = (bf16[384,576]{1,0:T(8,128)(2,1)}, bf16[384,576]{1,0:T(8,128)(2,1)S(1)}, u32[]{:S(2)}, u32[]{:S(2)}) collective-permute-start(bf16[384,576]{1,0:T(8,128)(2,1)} %get-tuple-element.31), channel_id=1, source_target_pairs={{0,240},{16,0},{32,16},{48,32},{64,48},{80,64},{96,80},{112,96},{1... | collective-permute-start | bytes 1327112 | tf_op jit(solution)/shard_map/ppermute | solution.py:104
  39.6 0.8 copy-start.5
  46.5 6.7 %collective-permute-start.5 = (bf16[384,576]{1,0:T(8,128)(2,1)}, bf16[384,576]{1,0:T(8,128)(2,1)S(1)}, u32[]{:S(2)}, u32[]{:S(2)}) collective-permute-start(bf16[384,576]{1,0:T(8,128)(2,1)} %get-tuple-element.36), channel_id=1, source_target_pairs={{0,240},{16,0},{32,16},{48,32},{64,48},{80,64},{96,80},{112,96},{1... | collective-permute-start | bytes 1327112 | tf_op jit(solution)/shard_map/ppermute | solution.py:104
  46.5 0.8 copy-start
  53.2 0.8 copy-start.1
  54.0 5.4 %copy-start.8 = (f32[1,576]{1,0:T(1,128)S(1)}, f32[1,576]{1,0:T(1,128)}, u32[]{:S(2)}) copy-start(f32[1,576]{1,0:T(1,128)} %get-tuple-element.48) | copy-start | bytes 6916
  54.0 5.4 %copy-start.9 = (f32[1,576]{1,0:T(1,128)S(1)}, f32[1,576]{1,0:T(1,128)}, u32[]{:S(2)}) copy-start(f32[1,576]{1,0:T(1,128)} %get-tuple-element.49) | copy-start | bytes 6916
  54.0 5.4 %copy-start.10 = (f32[1,576]{1,0:T(1,128)S(1)}, f32[1,576]{1,0:T(1,128)}, u32[]{:S(2)}) copy-start(f32[1,576]{1,0:T(1,128)} %get-tuple-element.50) | copy-start | bytes 6916
  76.0 1.0 copy-start.6
  76.0 1.2 copy-start.7
Sparse Core Ops, SparseCore 0:
  76.2 168.8 all-reduce.3

commit v2 on v1

v2 whole, which is shorter than its diff:
```python
import functools

import jax
import jax.numpy as jnp
from jax import lax
from jax.experimental import pallas as pl
from jax.experimental.pallas import tpu as pltpu
from jax.sharding import PartitionSpec as P

CUTS = (0, 512, 768)
LANES = 128

epsilon = 1e-05
bf16 = jnp.bfloat16
f32 = jnp.float32


def mul(a, b):
    return lax.dot_general(a, b, (((1,), (0,)), ((), ())), preferred_element_type=f32)


def mul_nt(a, b):
    return lax.dot_general(a, b, (((1,), (1,)), ((), ())), preferred_element_type=f32)


def column(row):
    return jnp.transpose(jnp.broadcast_to(row, (LANES, row.shape[1])))[:, :1]


def norm_parts(hidden):
    floated = hidden.astype(f32)
    inverse = lax.rsqrt(jnp.mean(floated * floated, axis=0, keepdims=True) + epsilon)
    return floated, inverse


def project(normed, gate_up_t):
    projected = mul(gate_up_t, normed)
    width = gate_up_t.shape[0] // 2
    gate_part = projected[:width]
    up_part = projected[width:]
    sig = jax.nn.sigmoid(gate_part)
    silu = gate_part * sig
    slope = up_part * sig * (1.0 + gate_part * (1.0 - sig))
    return (silu * up_part).astype(bf16), slope, silu


def back_through_norm(norm_grad, floated, inverse, outgrad, gain):
    product = norm_grad * floated * inverse
    size = product.shape[1]
    gain_term = functools.reduce(jnp.add, [product[:, i : i + LANES] for i in range(0, size, LANES)])
    scaled = norm_grad * gain
    inner = jnp.mean(scaled * floated, axis=0, keepdims=True)
    in_grad = outgrad.astype(f32) + inverse * (scaled - floated * (inverse * inverse * inner))
    return in_grad.astype(bf16), gain_term


def forward_kernel(span, first, *refs):
    tok_ref, gu_ref, dn_t_ref, gain_ref = refs[:4]
    next_ref, normed_ref, act_ref, slope_ref, silu_ref, *made = refs[4 if first else 5 :]
    if first:
        gu_t_ref, dn_ref = made
        gu_t_ref[...] = jnp.transpose(gu_ref[...])
        dn_ref[...] = jnp.transpose(dn_t_ref[...])
    else:
        gu_t_ref = gu_ref
    floated, inverse = norm_parts(tok_ref[:, span[0] : span[1]])
    normed = (floated * inverse * column(gain_ref[...])).astype(bf16)
    normed_ref[...] = normed
    activated, slope, silu = project(normed, gu_t_ref[...])
    act_ref[...] = activated
    slope_ref[...] = slope.astype(bf16)
    silu_ref[...] = silu.astype(bf16)
    next_ref[...] = (floated + mul(dn_t_ref[...], activated)).astype(bf16)


def turn_kernel(span, h_ref, out_ref, gu_t_ref, gu_ref, dn_ref, gain_ref, _, in_ref, normed_ref, act_ref, mixed_ref, term_ref):
    outgrad = out_ref[:, span[0] : span[1]]
    gain = column(gain_ref[...])
    floated, inverse = norm_parts(h_ref[...])
    normed = (floated * inverse * gain).astype(bf16)
    normed_ref[...] = normed
    activated, slope, silu = project(normed, gu_t_ref[...])
    act_ref[...] = activated
    act_grad = mul(dn_ref[...], outgrad)
    mixed = jnp.concatenate([(act_grad * slope).astype(bf16), (act_grad * silu).astype(bf16)], axis=0)
    mixed_ref[...] = mixed
    norm_grad = mul(gu_ref[...], mixed)
    in_ref[...], term_ref[...] = back_through_norm(norm_grad, floated, inverse, outgrad, gain)


def weight_kernel(spans, out_ref, *refs):
    count = len(spans)
    normed, mixed, acts, terms = [refs[i * count : (i + 1) * count] for i in range(4)]
    gu_ref, dn_ref, gain_ref = refs[4 * count :]
    gu_ref[...] = functools.reduce(jnp.add, [mul_nt(a[...], b[...]) for a, b in zip(normed, mixed)])
    dn_ref[...] = functools.reduce(jnp.add, [mul_nt(out_ref[:, lo:hi], a[...]) for (lo, hi), a in zip(spans, acts)])
    gain_ref[...] = functools.reduce(jnp.add, [t[...] for t in terms])


def backward_kernel(span, last, *refs):
    tok_ref, out_ref, slope_ref, silu_ref, normed_ref, act_ref, dn_ref, gu_ref, gain_ref = refs[:9]
    gu_sum_ref, dn_sum_ref, gain_sum_ref = refs[9:12]
    hid = dn_ref.shape[0]
    gain = column(gain_ref[...])
    outgrad = out_ref[...]
    act_grad = mul(dn_ref[...], outgrad)
    mixed = jnp.concatenate(
        [
            (act_grad * slope_ref[...].astype(f32)).astype(bf16),
            (act_grad * silu_ref[...].astype(f32)).astype(bf16),
        ],
        axis=0,
    )
    floated, inverse = norm_parts(tok_ref[:, span[0] : span[1]])
    norm_grad = mul(gu_ref[...], mixed)
    in_grad, term = back_through_norm(norm_grad, floated, inverse, outgrad, gain)
    gu_sum = gu_sum_ref[...] + mul_nt(normed_ref[...], mixed)
    dn_sum = dn_sum_ref[...] + mul_nt(outgrad, act_ref[...])
    gain_sum = gain_sum_ref[...] + term
    if last:
        before_ref, grad_ref, total_ref = refs[12:]
        grad_ref[:, : span[0]] = before_ref[...]
        grad_ref[:, span[0] : span[1]] = in_grad
        total_ref[:, : 2 * hid] = gu_sum.astype(bf16)
        total_ref[:, 2 * hid : 3 * hid] = dn_sum.astype(bf16)
        gain_col = jnp.sum(gain_sum, axis=1, keepdims=True)
        total_ref[:, 3 * hid :] = jnp.broadcast_to(gain_col, (gain_col.shape[0], 2 * LANES)).astype(bf16)
    else:
        in_ref, gu_out, dn_out, gain_out = refs[12:]
        in_ref[...] = in_grad
        gu_out[...] = gu_sum
        dn_out[...] = dn_sum
        gain_out[...] = gain_sum


def call(kernel, outs, args, aliases={}, kept=True):
    shaped = pltpu.VMEM if kept else jax.ShapeDtypeStruct
    inside = pl.BlockSpec(memory_space=pltpu.VMEM)
    return pl.pallas_call(
        kernel,
        out_shape=[shaped(shape, dtype) for shape, dtype in outs],
        in_specs=[inside] * len(args),
        out_specs=[inside] * len(outs),
        input_output_aliases=aliases,
        compiler_params=pltpu.CompilerParams(vmem_limit_bytes=24 * 2**20),
    )(*[pltpu.with_memory_space_constraint(a, pltpu.VMEM) for a in args])


def passed_along(x, axis, by):
    peers = lax.axis_size(axis)
    return lax.ppermute(x, axis, [(i, (i + by) % peers) for i in range(peers)])


def split_kernel(in_ref, gu_ref, dn_ref, gain_ref):
    wide, hid = gu_ref.shape[2], dn_ref.shape[2]
    gu_ref[...] = in_ref[:, :wide].astype(f32)[:, None, :]
    dn_ref[...] = in_ref[:, wide : wide + hid].astype(f32)[:, None, :]
    gains = in_ref[:, wide + hid : wide + hid + LANES].astype(f32)
    row = lax.broadcasted_iota(jnp.int32, gains.shape, 0)
    lane = lax.broadcasted_iota(jnp.int32, gains.shape, 1)
    gain_ref[...] = jnp.sum(jnp.where(row == lane, gains, 0.0), axis=0, keepdims=True)[:, : gain_ref.shape[1]]


def per_device(tokens, cotangent, gate_up, down_proj, norm_gain):
    tok, cot = tokens.T, cotangent.T
    gu, dn_t, gain = gate_up[0], down_proj[0].T, norm_gain
    width, rows = tok.shape
    hid = dn_t.shape[1]
    spans = list(zip(CUTS[:-1], CUTS[1:]))
    out = passed_along(cot, "blk", 1)
    kept, nexts, sent = [], [], []
    gu_t = dn = None
    for lo, hi in spans:
        n = hi - lo
        first = lo == 0
        shapes = [((width, n), bf16), ((width, n), bf16)] + [((hid, n), bf16)] * 3
        args = (tok, gu, dn_t, gain) if first else (tok, gu_t, dn_t, gain, out)
        if first:
            shapes += [((2 * hid, width), bf16), ((hid, width), bf16)]
        nxt, *parts = call(functools.partial(forward_kernel, (lo, hi), first), shapes, args)
        if first:
            *parts, gu_t, dn = parts
        kept.append(parts)
        nexts.append(nxt)
        sent.append(passed_along(nxt, "blk", 1))
    turned, returned = [], []
    after = nexts[-1]
    for (lo, hi), hidden in zip(spans, sent):
        n = hi - lo
        in_grad, *parts = call(
            functools.partial(turn_kernel, (lo, hi)),
            [((width, n), bf16)] * 2 + [((hid, n), bf16), ((2 * hid, n), bf16), ((width, LANES), f32)],
            (hidden, out, gu_t, gu, dn, gain, after),
        )
        after = in_grad
        turned.append(parts)
        returned.append(passed_along(in_grad, "blk", -1))
    sums_shape = [((width, 2 * hid), f32), ((width, hid), f32), ((width, LANES), f32)]
    sums = call(
        functools.partial(weight_kernel, spans),
        sums_shape,
        [out] + [part[i] for i in (0, 2, 1, 3) for part in turned],
    )
    before = None
    for (lo, hi), back, (normed, act, slope, silu) in zip(spans, returned, kept):
        last = hi == rows
        args = (tok, back, slope, silu, normed, act, dn, gu, gain, *sums)
        kernel = functools.partial(backward_kernel, (lo, hi), last)
        if last:
            shapes = [((width, rows), bf16), ((width, 3 * hid + 2 * LANES), bf16)]
            grad, total = call(kernel, shapes, (*args, before))
        else:
            before, *sums = call(
                kernel, [((width, hi - lo), bf16)] + sums_shape, args, {9: 1, 10: 2, 11: 3}
            )
    mine = lax.psum_scatter(total, "rep", scatter_dimension=0, tiled=True)
    mine = lax.optimization_barrier(mine)
    share = mine.shape[0]
    gu_mine, dn_mine, gain_mine = call(
        split_kernel, [((share, 1, 2 * hid), f32), ((share, 1, hid), f32), ((1, share), f32)], (mine,), kept=False
    )
    return grad.T, gu_mine.transpose(1, 0, 2), dn_mine.transpose(1, 2, 0), gain_mine


def solution(mesh):
    placed = (
        P(("blk", "rep"), None),
        P(("blk", "rep"), None),
        P("blk", None, None),
        P("blk", None, None),
        P("blk", None),
    )
    return jax.shard_map(
        per_device,
        mesh=mesh,
        in_specs=placed,
        out_specs=(
            P(("blk", "rep"), None),
            P("blk", "rep", None),
            P("blk", None, "rep"),
            P("blk", "rep"),
        ),
        check_vma=False,
    )
```

time: 260 us -> 120 us (0.46)
  the two profiles are of different devices: /device:TPU:20 before, /device:TPU:38 now
where the time goes in v2:
time: 120 us; the launch traced here: 119 us
  blocking collectives  54.3 us (45%)
  waiting for transfers between devices  27.6 us (23%)
  Pallas kernels  21.2 us (18%)
  local copies, waits for them, and re-layouts  8.3 us (7%)
  starting transfers between devices  6.34 us (5%)
  between operations  1.48 us (1%)
    unnamed x1, blocking collectives  54.3 us
    pallas_call x8, Pallas kernels, call(): pl.pallas_call(kernel, out_shape=[shaped(shape, dtype) for shape, dtype i...  21.2 us
    ppermute x5, waiting for transfers between devices, passed_along(): return lax.ppermute(x, axis, [(i, (i + by) % peers) for i in range(peers)])  18.3 us
    unnamed x2, waiting for transfers between devices  9.32 us
    unnamed x23, local copies, waits for them, and re-layouts  8.3 us
    unnamed x2, starting transfers between devices  3.84 us
    ppermute x5, starting transfers between devices, passed_along(): return lax.ppermute(x, axis, [(i, (i + by) % peers) for i in range(peers)])  2.5 us
  transfers between devices with their start and end apart: 7, of which 4 were waited for; matrix products, arithmetic and copies ran while one was open for 1% of the time, Pallas kernels for 12%

profile of v2, /device:TPU:38, one launch (start us, length us, event | category | flops | bytes accessed | tf_op | source)
XLA Modules:
  0.0 119.3 jit_solution(16263612175263787631)
XLA Ops:
  0.6 0.1 collective-permute-start
  0.7 0.0 copy-start
  0.7 1.5 %copy-done = bf16[1,576,1536]{2,1,0:T(8,128)(2,1)S(1)} copy-done((bf16[1,576,1536]{2,1,0:T(8,128)(2,1)S(1)}, bf16[1,576,1536]{2,1,0:T(8,128)(2,1)}, u32[]{:S(2)}) %copy-start) | copy-done | bytes 1769496
  2.2 0.0 copy-start.2
  2.2 1.2 copy-done.2
  3.4 0.0 copy-start.4
  3.4 1.2 copy-done.4
  4.5 0.0 copy-start.6
  4.5 0.7 copy-done.6
  5.2 2.7 %shard_map.84 = (bf16[576,512]{1,0:T(8,128)(2,1)S(1)}, bf16[576,512]{1,0:T(8,128)(2,1)S(1)}, bf16[768,512]{1,0:T(8,128)(2,1)S(1)}, bf16[768,512]{1,0:T(8,128)(2,...) custom-call(bf16[576,768]{1,0:T(8,128)(2,1)S(1)} %bitcast.18, ...), custom_call_target="tpu_custom_call" | custom-call | tf_op jit(solution)/shard_map/pallas_call | solution.py:139
  7.9 0.0 copy-start.1
  7.9 0.0 copy-start.7
  7.9 1.8 %collective-permute-start.2 = (bf16[576,512]{1,0:T(8,128)(2,1)S(1)}, bf16[576,512]{1,0:T(8,128)(2,1)S(1)}, u32[]{:S(2)}, u32[]{:S(2)}) collective-permute-start(bf16[576,512]{1,0:T(8,128)(2,1)S(1)} %get-tuple-element.41), channel_id=1, source_target_pairs={{0,16},{16,32},{32,48},{48,64},{64,80},{80,96},{96,112},{112,128},... | collective-permute-start | bytes 1769480 | tf_op jit(solution)/shard_map/ppermute | solution.py:151
  9.7 5.8 %collective-permute-done.refs_4_.out_ref = bf16[576,768]{1,0:T(8,128)(2,1)S(1)} collective-permute-done((bf16[576,768]{1,0:T(8,128)(2,1)}, bf16[576,768]{1,0:T(8,128)(2,1)S(1)}, u32[]{:S(2)}, u32[]{:S(2)}) %collective-permute-start) | collective-permute-done | bytes 884768 | tf_op jit(solution)/shard_map/ppermute | solution.py:151
  15.5 1.9 %shard_map.85 = (bf16[576,256]{1,0:T(8,128)(2,1)S(1)}, bf16[576,256]{1,0:T(8,128)(2,1)S(1)}, bf16[768,256]{1,0:T(8,128)(2,1)S(1)}, bf16[768,256]{1,0:T(8,128)(2,1)S(1)}, bf16[768,256]{1,0:T(8,128)(2,1)S(1)}) custom-call(bf16[576,768]{1,0:T(8,128)(2,1)S(1)} %bitcast.19, bf16[1536,576]{1,0:T(8,128)(2,1)S(1)} %get-tuple-element.38.refs_1_.gu_t_ref, ...), custom_call_target="tpu_custom_call" | custom-call | tf_op jit(solution)/shard_map/pallas_call | solution.py:139
  17.4 4.5 %collective-permute-done.2.h_ref = bf16[576,512]{1,0:T(8,128)(2,1)S(1)} collective-permute-done((bf16[576,512]{1,0:T(8,128)(2,1)S(1)}, bf16[576,512]{1,0:T(8,128)(2,1)S(1)}, u32[]{:S(2)}, u32[]{:S(2)}) %collective-permute-start.2) | collective-permute-done | bytes 589856 | tf_op jit(solution)/shard_map/ppermute | solution.py:151
  21.8 0.0 copy-done.1
  21.8 0.0 copy-done.7
  21.8 4.0 %shard_map.86 = (bf16[576,512]{1,0:T(8,128)(2,1)S(1)}, bf16[576,512]{1,0:T(8,128)(2,1)S(1)}, bf16[768,512]{1,0:T(8,128)(2,1)S(1)}, bf16[1536,512]{1,0:T(8,128)(2,1)S(1)}, f32[576,128]{1,0:T(8,128)S(1)}) custom-call(bf16[576,512]{1,0:T(8,128)(2,1)S(1)} %collective-permute-done.2.h_ref, bf16[576,768]{1,0:T(8,128)(2,1)S(1)} %collective-permute-done.refs_4_.out_ref, ...), custom_call_target="tpu_custom_call" | custom-call | tf_op jit(solution)/shard_map/pallas_call | solution.py:139
  25.8 0.1 collective-permute-start.4
  25.9 0.5 collective-permute-start.1
  26.4 8.0 %collective-permute-done.1.h_ref = bf16[576,256]{1,0:T(8,128)(2,1)S(1)} collective-permute-done((bf16[576,256]{1,0:T(8,128)(2,1)S(1)}, bf16[576,256]{1,0:T(8,128)(2,1)S(1)}, u32[]{:S(2)}, u32[]{:S(2)}) %collective-permute-start.1) | collective-permute-done | bytes 294944 | tf_op jit(solution)/shard_map/ppermute | solution.py:151
  34.4 3.0 %shard_map.87 = (bf16[576,256]{1,0:T(8,128)(2,1)S(1)}, bf16[576,256]{1,0:T(8,128)(2,1)S(1)}, bf16[768,256]{1,0:T(8,128)(2,1)S(1)}, bf16[1536,256]{1,0:T(8,128)(2,1)S(1)}, f32[576,128]{1,0:T(8,128)S(1)}) custom-call(bf16[576,256]{1,0:T(8,128)(2,1)S(1)} %collective-permute-done.1.h_ref, bf16[576,768]{1,0:T(8,128)(2,1)S(1)} %collective-permute-done.refs_4_.out_ref, ...), custom_call_target="tpu_custom_call" | custom-call | tf_op jit(solution)/shard_map/pallas_call | solution.py:139
  37.4 0.1 collective-permute-start.3
  37.5 0.0 copy-start.3
  37.5 2.3 %shard_map.88 = (f32[576,1536]{1,0:T(8,128)S(1)}, f32[576,768]{1,0:T(8,128)S(1)}, f32[576,128]{1,0:T(8,128)S(1)}) custom-call(bf16[576,768]{1,0:T(8,128)(2,1)S(1)} %collective-permute-done.refs_4_.out_ref, bf16[576,512]{1,0:T(8,128)(2,1)S(1)} %get-tuple-element.52.refs_0_, bf16[576,256]{1,0:T(8,128)(2,1)S(1)} %get-tuple-element.53.refs_1_, ...), custom_call_target="tpu_custom_call" | custom-call | tf_op jit(solution)/shard_map/pallas_call | solution.py:139
  39.8 0.0 collective-permute-done.4.refs_1_
  39.8 0.0 copy-done.3
  39.8 4.2 %shard_map.89 = (bf16[576,512]{1,0:T(8,128)(2,1)S(1)}, f32[576,1536]{1,0:T(8,128)S(1)}, f32[576,768]{1,0:T(8,128)S(1)}, f32[576,128]{1,0:T(8,128)S(1)}) custom-call(bf16[576,768]{1,0:T(8,128)(2,1)S(1)} %bitcast.20, bf16[576,512]{1,0:T(8,128)(2,1)S(1)} %collective-permute-done.4.refs_1_, ...), custom_call_target="tpu_custom_call", output_to_operand_aliasing={{1}: (9, {}), {2}: (10, {}), {3}: (11, {})} | custom-call | tf_op jit(solution)/shard_map/pallas_call | solution.py:139
  44.1 0.0 collective-permute-done.3.refs_1_
  44.1 2.5 %shard_map.90 = (bf16[576,768]{1,0:T(8,128)(2,1)S(1)}, bf16[576,2560]{1,0:T(8,128)(2,1)S(1)}) custom-call(bf16[576,768]{1,0:T(8,128)(2,1)S(1)} %bitcast.21, bf16[576,256]{1,0:T(8,128)(2,1)S(1)} %collective-permute-done.3.refs_1_, bf16[768,256]{1,0:T(8,128)(2,1)S(1)} %get-tuple-element.44.refs_2_, bf16[768,256]{1,0:T(8,128)(2,1)S(1)} %get-tuple-element.45.refs_3_, ...), custom_call_target="tpu_custom_call" | custom-call | tf_op jit(solution)/shard_map/pallas_call | solution.py:139
  46.6 0.0 copy-start.5
  46.6 1.6 %copy-done.5 = bf16[576,2560]{1,0:T(8,128)(2,1)} copy-done((bf16[576,2560]{1,0:T(8,128)(2,1)}, bf16[576,2560]{1,0:T(8,128)(2,1)S(1)}, u32[]{:S(2)}) %copy-start.5) | copy-done | bytes 2949144
  48.1 0.0 copy-start.8
  48.1 54.3 %fusion = bf16[40,2560]{1,0:T(8,128)(2,1)S(1)} fusion(bf16[576,2560]{1,0:T(8,128)(2,1)} %copy-done.5), kind=kCustom, calls=%all-reduce-scatter | all-reduce-scatter fusion | flops 1638401 | bytes 3154944
  102.4 1.9 %collective-permute-start.5 = (bf16[40,2560]{1,0:T(8,128)(2,1)S(1)}, bf16[40,2560]{1,0:T(8,128)(2,1)S(1)}, u32[]{:S(2)}, u32[]{:S(2)}) collective-permute-start(bf16[40,2560]{1,0:T(8,128)(2,1)S(1)} %fusion), channel_id=1, source_target_pairs={{0,1},{1,2},{2,3},{3,4},{4,5},{5,6},{6,7},{7,8},{8,9},{9,10},{10,1... | collective-permute-start | bytes 614408
  104.4 1.9 %collective-permute-start.6 = (bf16[20,2560]{1,0:T(8,128)(2,1)S(1)}, bf16[20,2560]{1,0:T(8,128)(2,1)S(1)}, u32[]{:S(2)}, u32[]{:S(2)}) collective-permute-start(bf16[20,2560]{1,0:T(8,128)(2,1)S(1)} %slice), channel_id=1, source_target_pairs={{0,2},{1,3},{2,4},{3,5},{4,6},{5,7},{6,8},{7,9},{8,10},{9,11},{10,... | collective-permute-start | bytes 307208
  106.3 0.0 copy-done.8
  106.3 0.6 dynamic-slice.4
  107.6 0.9 copy.15
  108.5 9.3 %collective-permute-done.6 = bf16[20,2560]{1,0:T(8,128)(2,1)S(1)} collective-permute-done((bf16[20,2560]{1,0:T(8,128)(2,1)S(1)}, bf16[20,2560]{1,0:T(8,128)(2,1)S(1)}, u32[]{:S(2)}, u32[]{:S(2)}) %collective-permute-start.6) | collective-permute-done | bytes 102432
  117.8 0.0 collective-permute-done.5
  117.8 0.6 concatenate
  118.5 0.1 constant_dynamic-slice_fusion.in_ref
  118.5 0.8 shard_map.91
  (1 shorter events, 0.0 us)
Async XLA Ops:
  0.6 14.9 %collective-permute-start = (bf16[576,768]{1,0:T(8,128)(2,1)}, bf16[576,768]{1,0:T(8,128)(2,1)S(1)}, u32[]{:S(2)}, u32[]{:S(2)}) collective-permute-start(bf16[576,768]{1,0:T(8,128)(2,1)} %bitcast.24), channel_id=1, source_target_pairs={{0,16},{16,32},{32,48},{48,64},{64,80},{80,96},{96,112},{112,128},... | collective-permute-start | bytes 2654216 | tf_op jit(solution)/shard_map/ppermute | solution.py:151
  0.7 1.5 %copy-start = (bf16[1,576,1536]{2,1,0:T(8,128)(2,1)S(1)}, bf16[1,576,1536]{2,1,0:T(8,128)(2,1)}, u32[]{:S(2)}) copy-start(bf16[1,576,1536]{2,1,0:T(8,128)(2,1)} %param.7) | copy-start | bytes 5308420
  2.2 1.2 copy-start.2
  3.4 1.2 copy-start.4
  4.5 0.7 copy-start.6
  7.9 13.9 %copy-start.1 = (bf16[1,576,1536]{2,1,0:T(8,128)(2,1)S(1)}, bf16[1,576,1536]{2,1,0:T(8,128)(2,1)}, u32[]{:S(2)}) copy-start(bf16[1,576,1536]{2,1,0:T(8,128)(2,1)} %param.7) | copy-start | bytes 5308420
  7.9 13.9 %copy-start.7 = (f32[1,576]{1,0:T(1,128)S(1)}, f32[1,576]{1,0:T(1,128)}, u32[]{:S(2)}) copy-start(f32[1,576]{1,0:T(1,128)} %refs_8_.3) | copy-start | bytes 6916
  7.9 13.9 %collective-permute-start.2 = (bf16[576,512]{1,0:T(8,128)(2,1)S(1)}, bf16[576,512]{1,0:T(8,128)(2,1)S(1)}, u32[]{:S(2)}, u32[]{:S(2)}) collective-permute-start(bf16[576,512]{1,0:T(8,128)(2,1)S(1)} %get-tuple-element.41), channel_id=1, source_target_pairs={{0,16},{16,32},{32,48},{48,64},{64,80},{80,96},{96,112},{112,128},... | collective-permute-start | bytes 1769480 | tf_op jit(solution)/shard_map/ppermute | solution.py:151
  25.8 14.0 %collective-permute-start.4 = (bf16[576,512]{1,0:T(8,128)(2,1)S(1)}, bf16[576,512]{1,0:T(8,128)(2,1)S(1)}, u32[]{:S(2)}, u32[]{:S(2)}) collective-permute-start(bf16[576,512]{1,0:T(8,128)(2,1)S(1)} %get-tuple-element.42._), channel_id=1, source_target_pairs={{0,240},{16,0},{32,16},{48,32},{64,48},{80,64},{96,80},{112,96},{1... | collective-permute-start | bytes 1769480 | tf_op jit(solution)/shard_map/ppermute | solution.py:151
  25.9 8.5 %collective-permute-start.1 = (bf16[576,256]{1,0:T(8,128)(2,1)S(1)}, bf16[576,256]{1,0:T(8,128)(2,1)S(1)}, u32[]{:S(2)}, u32[]{:S(2)}) collective-permute-start(bf16[576,256]{1,0:T(8,128)(2,1)S(1)} %get-tuple-element.39._), channel_id=1, source_target_pairs={{0,16},{16,32},{32,48},{48,64},{64,80},{80,96},{96,112},{112,128},... | collective-permute-start | bytes 884744 | tf_op jit(solution)/shard_map/ppermute | solution.py:151
  37.4 6.7 %collective-permute-start.3 = (bf16[576,256]{1,0:T(8,128)(2,1)S(1)}, bf16[576,256]{1,0:T(8,128)(2,1)S(1)}, u32[]{:S(2)}, u32[]{:S(2)}) collective-permute-start(bf16[576,256]{1,0:T(8,128)(2,1)S(1)} %get-tuple-element.43), channel_id=1, source_target_pairs={{0,240},{16,0},{32,16},{48,32},{64,48},{80,64},{96,80},{112,96},{1... | collective-permute-start | bytes 884744 | tf_op jit(solution)/shard_map/ppermute | solution.py:151
  37.5 2.4 %copy-start.3 = (bf16[768,576]{0,1:T(8,128)(2,1)S(1)}, bf16[768,576]{0,1:T(8,128)(2,1)}, u32[]{:S(2)}) copy-start(bf16[768,576]{0,1:T(8,128)(2,1)} %param.5) | copy-start | bytes 2654212
  46.6 1.6 %copy-start.5 = (bf16[576,2560]{1,0:T(8,128)(2,1)}, bf16[576,2560]{1,0:T(8,128)(2,1)S(1)}, u32[]{:S(2)}) copy-start(bf16[576,2560]{1,0:T(8,128)(2,1)S(1)} %get-tuple-element.68) | copy-start | bytes 8847364
  48.1 58.2 %copy-start.8 = (u32[256]{0:T(256)S(1)}, u32[256]{0:T(256)}, u32[]{:S(2)}) copy-start(u32[256]{0:T(256)} %constant.5) | copy-start | bytes 3076
  102.4 15.4 %collective-permute-start.5 = (bf16[40,2560]{1,0:T(8,128)(2,1)S(1)}, bf16[40,2560]{1,0:T(8,128)(2,1)S(1)}, u32[]{:S(2)}, u32[]{:S(2)}) collective-permute-start(bf16[40,2560]{1,0:T(8,128)(2,1)S(1)} %fusion), channel_id=1, source_target_pairs={{0,1},{1,2},{2,3},{3,4},{4,5},{5,6},{6,7},{7,8},{8,9},{9,10},{10,1... | collective-permute-start | bytes 614408
  104.4 13.4 %collective-permute-start.6 = (bf16[20,2560]{1,0:T(8,128)(2,1)S(1)}, bf16[20,2560]{1,0:T(8,128)(2,1)S(1)}, u32[]{:S(2)}, u32[]{:S(2)}) collective-permute-start(bf16[20,2560]{1,0:T(8,128)(2,1)S(1)} %slice), channel_id=1, source_target_pairs={{0,2},{1,3},{2,4},{3,5},{4,6},{5,7},{6,8},{7,9},{8,10},{9,11},{10,... | collective-permute-start | bytes 307208

commit v3 on v2

v3 whole, which is shorter than its diff:
```python
import functools

import jax
import jax.numpy as jnp
from jax import lax
from jax.experimental import pallas as pl
from jax.experimental.pallas import tpu as pltpu
from jax.sharding import PartitionSpec as P

SPANS = ((0, 512), (512, 768))
LANES = 128
SHARE = 36
RING = 8
HALF = 656
SLOT = 1328
SHORT = SLOT - 2

epsilon = 1e-05
bf16 = jnp.bfloat16
f32 = jnp.float32


def mul(a, b):
    return lax.dot_general(a, b, (((1,), (0,)), ((), ())), preferred_element_type=f32)


def mul_nt(a, b):
    return lax.dot_general(a, b, (((1,), (1,)), ((), ())), preferred_element_type=f32)


def column(row):
    return jnp.transpose(jnp.broadcast_to(row, (LANES, row.shape[1])))[:, :1]


def norm_parts(hidden):
    floated = hidden.astype(f32)
    inverse = lax.rsqrt(jnp.mean(floated * floated, axis=0, keepdims=True) + epsilon)
    return floated, inverse


def project(normed, gate_up_t):
    projected = mul(gate_up_t, normed)
    width = gate_up_t.shape[0] // 2
    gate_part = projected[:width]
    up_part = projected[width:]
    sig = jax.nn.sigmoid(gate_part)
    silu = gate_part * sig
    slope = up_part * sig * (1.0 + gate_part * (1.0 - sig))
    return (silu * up_part).astype(bf16), slope, silu


def back_through_norm(norm_grad, floated, inverse, outgrad, gain):
    product = norm_grad * floated * inverse
    size = product.shape[1]
    gain_term = functools.reduce(jnp.add, [product[:, i : i + LANES] for i in range(0, size, LANES)])
    scaled = norm_grad * gain
    inner = jnp.mean(scaled * floated, axis=0, keepdims=True)
    in_grad = outgrad.astype(f32) + inverse * (scaled - floated * (inverse * inverse * inner))
    return in_grad.astype(bf16), gain_term


def forward_kernel(tok_ref, gu_ref, dn_t_ref, gain_ref, next_ref, normed_ref, act_ref, slope_ref, silu_ref, gu_t_ref, dn_ref):
    gu_t_ref[...] = jnp.transpose(gu_ref[...])
    dn_ref[...] = jnp.transpose(dn_t_ref[...])
    gain = column(gain_ref[...])
    for lo, hi in SPANS:
        floated, inverse = norm_parts(tok_ref[:, lo:hi])
        normed = (floated * inverse * gain).astype(bf16)
        normed_ref[:, lo:hi] = normed
        activated, slope, silu = project(normed, gu_t_ref[...])
        act_ref[:, lo:hi] = activated
        slope_ref[:, lo:hi] = slope.astype(bf16)
        silu_ref[:, lo:hi] = silu.astype(bf16)
        next_ref[:, lo:hi] = (floated + mul(dn_t_ref[...], activated)).astype(bf16)


def turn_kernel(span, h_ref, out_ref, gu_t_ref, gu_ref, dn_ref, gain_ref, _, in_ref, normed_ref, act_ref, mixed_ref, term_ref):
    outgrad = out_ref[:, span[0] : span[1]]
    gain = column(gain_ref[...])
    floated, inverse = norm_parts(h_ref[:, span[0] : span[1]])
    normed = (floated * inverse * gain).astype(bf16)
    normed_ref[...] = normed
    activated, slope, silu = project(normed, gu_t_ref[...])
    act_ref[...] = activated
    act_grad = mul(dn_ref[...], outgrad)
    mixed = jnp.concatenate([(act_grad * slope).astype(bf16), (act_grad * silu).astype(bf16)], axis=0)
    mixed_ref[...] = mixed
    norm_grad = mul(gu_ref[...], mixed)
    in_ref[...], term_ref[...] = back_through_norm(norm_grad, floated, inverse, outgrad, gain)


def weight_kernel(out_ref, *refs):
    count = len(SPANS)
    normed, mixed, acts, terms = [refs[i * count : (i + 1) * count] for i in range(4)]
    gu_ref, dn_ref, gain_ref = refs[4 * count :]
    gu_ref[...] = functools.reduce(jnp.add, [mul_nt(a[...], b[...]) for a, b in zip(normed, mixed)])
    dn_ref[...] = functools.reduce(jnp.add, [mul_nt(out_ref[:, lo:hi], a[...]) for (lo, hi), a in zip(SPANS, acts)])
    gain_ref[...] = functools.reduce(jnp.add, [t[...] for t in terms])


def fill_slots(slots_ref, staged_ref, total_ref, sems, gu_sum, dn_sum, gain_sum):
    gain_sum = jnp.broadcast_to(gain_sum, (gain_sum.shape[0], LANES))
    columns = [x[:, i : i + LANES] for x in (gu_sum, dn_sum) for i in range(0, x.shape[1], LANES)]
    tail = HALF - SHARE * len(columns)
    own = lax.broadcasted_iota(jnp.int32, (SHARE, LANES), 0) == lax.broadcasted_iota(jnp.int32, (SHARE, LANES), 1)
    top = lax.broadcasted_iota(jnp.int32, (tail, LANES), 0) == 0
    copies = []
    for place in range(RING):
        for half in range(2):
            first = (half * RING + place) * SHARE
            rows = slice(first, first + SHARE)
            at = place * SLOT + half * HALF
            for column_block in columns:
                slots_ref[at : at + SHARE] = column_block[rows]
                at += SHARE
            gains = jnp.sum(jnp.where(own, gain_sum[rows], 0.0), axis=0, keepdims=True)
            slots_ref[at : at + tail] = jnp.where(top, gains, 0.0)
        low = place * SLOT
        if place < RING - 1:
            slots_ref[low + 2 * HALF : low + SLOT] = jnp.zeros((SLOT - 2 * HALF, LANES), f32)
            high = low + SLOT
        else:
            high = low + 2 * HALF
        staged_ref[low:high] = slots_ref[low:high].astype(bf16)
        copy = pltpu.make_async_copy(staged_ref.at[low:high], total_ref.at[low:high], sems.at[place])
        copy.start()
        copies.append(copy)
    for copy in copies:
        copy.wait()


def touch_kernel(out_ref, next_ref, seen_ref):
    seen_ref[...] = out_ref[:16, :LANES] + next_ref[:16, :LANES]


def backward_kernel(span, last, *refs):
    tok_ref, out_ref, slope_ref, silu_ref, normed_ref, act_ref, dn_ref, gu_ref, gain_ref = refs[:9]
    part = (slice(None), slice(*span))
    gu_sum_ref, dn_sum_ref, gain_sum_ref = refs[9:12]
    hid = dn_ref.shape[0]
    gain = column(gain_ref[...])
    outgrad = out_ref[...]
    act_grad = mul(dn_ref[...], outgrad)
    mixed = jnp.concatenate(
        [
            (act_grad * slope_ref[part].astype(f32)).astype(bf16),
            (act_grad * silu_ref[part].astype(f32)).astype(bf16),
        ],
        axis=0,
    )
    floated, inverse = norm_parts(tok_ref[part])
    norm_grad = mul(gu_ref[...], mixed)
    in_grad, term = back_through_norm(norm_grad, floated, inverse, outgrad, gain)
    gu_sum = gu_sum_ref[...] + mul_nt(normed_ref[part], mixed)
    dn_sum = dn_sum_ref[...] + mul_nt(outgrad, act_ref[part])
    gain_sum = gain_sum_ref[...] + term
    if last:
        before_ref, grad_ref, total_ref, slots_ref, staged_ref, sems = refs[12:]
        grad_ref[:, : span[0]] = before_ref[...]
        grad_ref[:, span[0] : span[1]] = in_grad
        gain_sum = jnp.sum(gain_sum, axis=1, keepdims=True)
        fill_slots(slots_ref, staged_ref, total_ref, sems, gu_sum, dn_sum, gain_sum)
    else:
        in_ref, gu_out, dn_out, gain_out = refs[12:]
        in_ref[...] = in_grad
        gu_out[...] = gu_sum
        dn_out[...] = dn_sum
        gain_out[...] = gain_sum


def call(kernel, outs, args, aliases={}, kept=True, scratch=(), free=0):
    shaped = pltpu.VMEM if kept else jax.ShapeDtypeStruct
    inside = pl.BlockSpec(memory_space=pltpu.VMEM)
    held = len(outs) - free
    return pl.pallas_call(
        kernel,
        out_shape=[shaped(*o) for o in outs[:held]] + [jax.ShapeDtypeStruct(*o) for o in outs[held:]],
        in_specs=[inside] * len(args),
        out_specs=[inside] * held + [pl.BlockSpec(memory_space=pl.ANY)] * free,
        input_output_aliases=aliases,
        scratch_shapes=scratch,
        compiler_params=pltpu.CompilerParams(vmem_limit_bytes=28 * 2**20),
    )(*[pltpu.with_memory_space_constraint(a, pltpu.VMEM) for a in args])


def passed_along(x, axis, by):
    peers = lax.axis_size(axis)
    return lax.ppermute(x, axis, [(i, (i + by) % peers) for i in range(peers)])


def split_kernel(in_ref, other_ref, gu_ref, dn_ref, gain_ref):
    at = 0
    got = in_ref[...].astype(f32) + other_ref[...].astype(f32)
    for ref in (gu_ref, dn_ref):
        for i in range(0, ref.shape[2], LANES):
            ref[:, :, i : i + LANES] = got[at : at + SHARE][:, None, :]
            at += SHARE
    gain_ref[...] = got[at : at + 1, :SHARE]


def per_device(tokens, cotangent, gate_up, down_proj, norm_gain):
    tok, cot = tokens.T, cotangent.T
    gu, dn_t, gain = gate_up[0], down_proj[0].T, norm_gain
    width, rows = tok.shape
    hid = dn_t.shape[1]
    length = RING * SHORT
    out = passed_along(cot, "blk", 1)
    wide = [((n, rows), bf16) for n in (width, width, hid, hid, hid)]
    nxt, normed, act, slope, silu, gu_t, dn = call(
        forward_kernel, wide + [((2 * hid, width), bf16), ((hid, width), bf16)], (tok, gu, dn_t, gain)
    )
    hidden = passed_along(nxt, "blk", 1)
    turned, returned = [], []
    (after,) = call(touch_kernel, [((16, LANES), bf16)], (out, nxt))
    for lo, hi in SPANS:
        n = hi - lo
        in_grad, *parts = call(
            functools.partial(turn_kernel, (lo, hi)),
            [((width, n), bf16)] * 2 + [((hid, n), bf16), ((2 * hid, n), bf16), ((width, LANES), f32)],
            (hidden, out, gu_t, gu, dn, gain, after),
        )
        after = in_grad
        turned.append(parts)
        returned.append(passed_along(in_grad, "blk", -1))
    sums_shape = [((width, 2 * hid), f32), ((width, hid), f32), ((width, LANES), f32)]
    sums = call(
        weight_kernel,
        sums_shape,
        [out] + [part[i] for i in (0, 2, 1, 3) for part in turned],
    )
    before = None
    for (lo, hi), back in zip(SPANS, returned):
        last = hi == rows
        args = (tok, back, slope, silu, normed, act, dn, gu, gain, *sums)
        kernel = functools.partial(backward_kernel, (lo, hi), last)
        if last:
            shapes = [((width, rows), bf16), ((length, LANES), bf16)]
            scratch = [pltpu.VMEM((length, LANES), f32), pltpu.VMEM((length, LANES), bf16), pltpu.SemaphoreType.DMA((RING,))]
            grad, total = call(kernel, shapes, (*args, before), scratch=scratch, free=1)
        else:
            before, *sums = call(
                kernel, [((width, hi - lo), bf16)] + sums_shape, args, {9: 1, 10: 2, 11: 3}
            )
    rings = [[half * RING + place for place in range(RING)] for half in range(2)]
    share = lax.psum_scatter(total, "rep", scatter_dimension=0, axis_index_groups=rings, tiled=True)
    share = lax.optimization_barrier(share)
    at = lax.axis_index("rep")
    half, start = at // RING, (at % RING) * (SLOT - SHORT)
    theirs = lax.dynamic_slice_in_dim(share, start + (1 - half) * HALF, HALF, 0)
    theirs = lax.ppermute(theirs, "rep", [(i, (i + RING) % (2 * RING)) for i in range(2 * RING)])
    mine = lax.dynamic_slice_in_dim(share, start + half * HALF, HALF, 0)
    gu_mine, dn_mine, gain_mine = call(
        split_kernel,
        [((SHARE, 1, 2 * hid), f32), ((SHARE, 1, hid), f32), ((1, SHARE), f32)],
        (mine, theirs),
        kept=False,
    )
    return grad.T, gu_mine.transpose(1, 0, 2), dn_mine.transpose(1, 2, 0), gain_mine


def solution(mesh):
    placed = (
        P(("blk", "rep"), None),
        P(("blk", "rep"), None),
        P("blk", None, None),
        P("blk", None, None),
        P("blk", None),
    )
    return jax.shard_map(
        per_device,
        mesh=mesh,
        in_specs=placed,
        out_specs=(
            P(("blk", "rep"), None),
            P("blk", "rep", None),
            P("blk", None, "rep"),
            P("blk", "rep"),
        ),
        check_vma=False,
    )
```

time: 120 us -> 99.4 us (0.83)
  the two profiles are of different devices: /device:TPU:38 before, /device:TPU:20 now
where the time goes in v3:
time: 99.4 us; the launch traced here: 99.1 us
  blocking collectives  40.8 us (41%)
  Pallas kernels  21.8 us (22%)
  waiting for transfers between devices  19.8 us (20%)
  local copies, waits for them, and re-layouts  9.03 us (9%)
  starting transfers between devices  6.22 us (6%)
  between operations  1.48 us (1%)
    unnamed x1, blocking collectives  40.8 us
    pallas_call x8, Pallas kernels, call(): pl.pallas_call(kernel, out_shape=[shaped(*o) for o in outs[:held]] + [jax...  21.8 us
    ppermute x4, waiting for transfers between devices, passed_along(): return lax.ppermute(x, axis, [(i, (i + by) % peers) for i in range(peers)])  13.7 us
    unnamed x23, local copies, waits for them, and re-layouts  8.92 us
    ppermute x1, waiting for transfers between devices, per_device(): lax.ppermute(theirs, 'rep', [(i, (i + RING) % (2 * RING)) for i in range(...  6.08 us
    unnamed x1, starting transfers between devices  3.2 us
    ppermute x4, starting transfers between devices, passed_along(): return lax.ppermute(x, axis, [(i, (i + by) % peers) for i in range(peers)])  2.43 us
  transfers between devices with their start and end apart: 6, of which 4 were waited for; matrix products, arithmetic and copies ran while one was open for 2% of the time, Pallas kernels for 13%

profile of v3, /device:TPU:20, one launch (start us, length us, event | category | flops | bytes accessed | tf_op | source)
XLA Modules:
  0.0 99.1 jit_solution(13778260373110407413)
XLA Ops:
  0.6 0.1 collective-permute-start.1
  0.7 0.0 copy-start
  0.7 1.5 %copy-done = bf16[1,576,1536]{2,1,0:T(8,128)(2,1)S(1)} copy-done((bf16[1,576,1536]{2,1,0:T(8,128)(2,1)S(1)}, bf16[1,576,1536]{2,1,0:T(8,128)(2,1)}, u32[]{:S(2)}) %copy-start) | copy-done | bytes 1769496
  2.2 0.0 copy-start.2
  2.2 1.2 %copy-done.2 = bf16[768,576]{0,1:T(8,128)(2,1)S(1)} copy-done((bf16[768,576]{0,1:T(8,128)(2,1)S(1)}, bf16[768,576]{0,1:T(8,128)(2,1)}, u32[]{:S(2)}) %copy-start.2) | copy-done | bytes 884760
  3.4 0.0 copy-start.5
  3.4 1.2 %copy-done.5 = bf16[1,768,576]{1,2,0:T(8,128)(2,1)S(1)} copy-done((bf16[1,768,576]{1,2,0:T(8,128)(2,1)S(1)}, bf16[1,768,576]{1,2,0:T(8,128)(2,1)}, u32[]{:S(2)}) %copy-start.5) | copy-done | bytes 884760
  4.5 0.0 copy-start.6
  4.5 0.7 copy-done.6
  5.2 0.0 copy-start.1
  5.2 3.9 %shard_map.84 = (bf16[576,768]{1,0:T(8,128)(2,1)S(1)}, bf16[576,768]{1,0:T(8,128)(2,1)S(1)}, bf16[768,768]{1,0:T(8,128)(2,1)S(1)}, bf16[768,768]{1,0:T(8,128)(2,...) custom-call(bf16[576,768]{1,0:T(8,128)(2,1)S(1)} %bitcast.18, ...), custom_call_target="tpu_custom_call" | custom-call | tf_op jit(solution)/shard_map/pallas_call | solution.py:175
  9.2 1.5 %collective-permute-start = (bf16[576,768]{1,0:T(8,128)(2,1)S(1)}, bf16[576,768]{1,0:T(8,128)(2,1)S(1)}, u32[]{:S(2)}, u32[]{:S(2)}) collective-permute-start(bf16[576,768]{1,0:T(8,128)(2,1)S(1)} %get-tuple-element.33.next_ref), channel_id=1, source_target_pairs={{0,16},{16,32},{32,48},{48,64},{64,80},{80,96},{96,112},{112,128},... | collective-permute-start | bytes 2654216 | tf_op jit(solution)/shard_map/ppermute | solution.py:188
  10.6 2.8 %collective-permute-done.1.out_ref = bf16[576,768]{1,0:T(8,128)(2,1)S(1)} collective-permute-done((bf16[576,768]{1,0:T(8,128)(2,1)}, bf16[576,768]{1,0:T(8,128)(2,1)S(1)}, u32[]{:S(2)}, u32[]{:S(2)}) %collective-permute-start.1) | collective-permute-done | bytes 884768 | tf_op jit(solution)/shard_map/ppermute | solution.py:188
  13.4 9.5 %collective-permute-done.h_ref = bf16[576,768]{1,0:T(8,128)(2,1)S(1)} collective-permute-done((bf16[576,768]{1,0:T(8,128)(2,1)S(1)}, bf16[576,768]{1,0:T(8,128)(2,1)S(1)}, u32[]{:S(2)}, u32[]{:S(2)}) %collective-permute-start) | collective-permute-done | bytes 884768 | tf_op jit(solution)/shard_map/ppermute | solution.py:188
  22.9 0.0 copy-done.1
  22.9 3.9 %shard_map.86 = (bf16[576,512]{1,0:T(8,128)(2,1)S(1)}, bf16[576,512]{1,0:T(8,128)(2,1)S(1)}, bf16[768,512]{1,0:T(8,128)(2,1)S(1)}, bf16[1536,512]{1,0:T(8,128)(2,1)S(1)}, f32[576,128]{1,0:T(8,128)S(1)}) custom-call(bf16[576,768]{1,0:T(8,128)(2,1)S(1)} %collective-permute-done.h_ref, bf16[576,768]{1,0:T(8,128)(2,1)S(1)} %collective-permute-done.1.out_ref, ...), custom_call_target="tpu_custom_call" | custom-call | tf_op jit(solution)/shard_map/pallas_call | solution.py:175
  26.7 0.1 collective-permute-start.3
  26.8 2.9 %shard_map.87 = (bf16[576,256]{1,0:T(8,128)(2,1)S(1)}, bf16[576,256]{1,0:T(8,128)(2,1)S(1)}, bf16[768,256]{1,0:T(8,128)(2,1)S(1)}, bf16[1536,256]{1,0:T(8,128)(2,1)S(1)}, f32[576,128]{1,0:T(8,128)S(1)}) custom-call(bf16[576,768]{1,0:T(8,128)(2,1)S(1)} %collective-permute-done.h_ref, bf16[576,768]{1,0:T(8,128)(2,1)S(1)} %collective-permute-done.1.out_ref, ...), custom_call_target="tpu_custom_call" | custom-call | tf_op jit(solution)/shard_map/pallas_call | solution.py:175
  29.7 0.8 collective-permute-start.2
  30.5 0.0 copy-start.3
  30.5 2.3 %shard_map.88 = (f32[576,1536]{1,0:T(8,128)S(1)}, f32[576,768]{1,0:T(8,128)S(1)}, f32[576,128]{1,0:T(8,128)S(1)}) custom-call(bf16[576,768]{1,0:T(8,128)(2,1)S(1)} %collective-permute-done.1.out_ref, bf16[576,512]{1,0:T(8,128)(2,1)S(1)} %get-tuple-element.42.refs_0_, bf16[576,256]{1,0:T(8,128)(2,1)S(1)} %get-tuple-element.43.refs_1_, ...), custom_call_target="tpu_custom_call" | custom-call | tf_op jit(solution)/shard_map/pallas_call | solution.py:175
  32.8 1.4 %collective-permute-done.3.refs_1_ = bf16[576,512]{1,0:T(8,128)(2,1)S(1)} collective-permute-done((bf16[576,512]{1,0:T(8,128)(2,1)S(1)}, bf16[576,512]{1,0:T(8,128)(2,1)S(1)}, u32[]{:S(2)}, u32[]{:S(2)}) %collective-permute-start.3) | collective-permute-done | bytes 589856 | tf_op jit(solution)/shard_map/ppermute | solution.py:188
  34.2 0.0 copy-done.3
  34.2 0.0 copy-start.7
  34.2 4.1 %shard_map.89 = (bf16[576,512]{1,0:T(8,128)(2,1)S(1)}, f32[576,1536]{1,0:T(8,128)S(1)}, f32[576,768]{1,0:T(8,128)S(1)}, f32[576,128]{1,0:T(8,128)S(1)}) custom-call(bf16[576,768]{1,0:T(8,128)(2,1)S(1)} %bitcast.19, bf16[576,512]{1,0:T(8,128)(2,1)S(1)} %collective-permute-done.3.refs_1_, ...), custom_call_target="tpu_custom_call", output_to_operand_aliasing={{1}: (9, {}), {2}: (10, {}), {3}: (11, {})} | custom-call | tf_op jit(solution)/shard_map/pallas_call | solution.py:175
  38.3 0.0 collective-permute-done.2.refs_1_
  38.3 0.0 copy-done.7
  38.3 3.9 %shard_map.90 = (bf16[576,768]{1,0:T(8,128)(2,1)S(1)}, bf16[10608,128]{1,0:T(8,128)(2,1)S(1)}) custom-call(bf16[576,768]{1,0:T(8,128)(2,1)S(1)} %bitcast.20, bf16[576,256]{1,0:T(8,128)(2,1)S(1)} %collective-permute-done.2.refs_1_, bf16[768,768]{1,0:T(8,128)(2,1)S(1)} %get-tuple-element.38.refs_2_, bf16[768,768]{1,0:T(8,128)(2,1)S(1)} %get-tuple-element.39.refs_3_, ...), custom_call_target="tpu_custom_call" | custom-call | tf_op jit(solution)/shard_map/pallas_call | solution.py:175
  42.2 0.0 copy-start.4
  42.2 1.5 %copy-done.4 = bf16[10608,128]{1,0:T(8,128)(2,1)} copy-done((bf16[10608,128]{1,0:T(8,128)(2,1)}, bf16[10608,128]{1,0:T(8,128)(2,1)S(1)}, u32[]{:S(2)}) %copy-start.4) | copy-done | bytes 2715672
  43.8 0.0 copy-start.8
  43.8 40.8 %fusion = bf16[1328,128]{1,0:T(8,128)(2,1)S(1)} fusion(bf16[10608,128]{1,0:T(8,128)(2,1)} %copy-done.4), kind=kCustom, calls=%all-reduce-scatter | all-reduce-scatter fusion | flops 1359873 | bytes 3056640
  84.6 3.2 %collective-permute-start.5 = (bf16[14,128]{1,0:T(8,128)(2,1)S(1)}, bf16[14,128]{1,0:T(8,128)(2,1)S(1)}, u32[]{:S(2)}, u32[]{:S(2)}) collective-permute-start(bf16[14,128]{1,0:T(8,128)(2,1)S(1)} %slice), channel_id=1, source_target_pairs={{0,1},{1,2},{2,3},{3,4},{4,5},{5,6},{6,7},{8,9},{9,10},{10,11},{11... | collective-permute-start | bytes 10760
  87.8 0.0 copy-done.8
  87.8 0.6 dynamic-slice.4
  89.1 0.0 collective-permute-done.5
  89.1 1.3 %concatenate = bf16[1342,128]{1,0:T(8,128)(2,1)S(1)} concatenate(bf16[14,128]{1,0:T(8,128)(2,1)S(1)} %collective-permute-done.5, bf16[1328,128]{1,0:T(8,128)(2,1)S(1)} %fusion), dimensions={0} | concatenate | bytes 687104
  90.4 0.1 constant_dynamic-slice_fusion
  90.5 0.1 constant_dynamic-slice_fusion.1
  90.6 0.6 collective-permute-start.4
  91.2 0.9 copy.15
  92.1 6.1 %collective-permute-done.4.other_ref = bf16[656,128]{1,0:T(8,128)(2,1)S(1)} collective-permute-done((bf16[656,128]{1,0:T(8,128)(2,1)S(1)}, bf16[656,128]{1,0:T(8,128)(2,1)S(1)}, u32[]{:S(2)}, u32[]{:S(2)}) %collective-permute-start.4) | collective-permute-done | bytes 167968 | tf_op jit(solution)/shard_map/ppermute | solution.py:250
  98.2 0.9 shard_map.91
  (2 shorter events, 0.0 us)
Async XLA Ops:
  0.6 12.8 %collective-permute-start.1 = (bf16[576,768]{1,0:T(8,128)(2,1)}, bf16[576,768]{1,0:T(8,128)(2,1)S(1)}, u32[]{:S(2)}, u32[]{:S(2)}) collective-permute-start(bf16[576,768]{1,0:T(8,128)(2,1)} %bitcast.22), channel_id=1, source_target_pairs={{0,16},{16,32},{32,48},{48,64},{64,80},{80,96},{96,112},{112,128},... | collective-permute-start | bytes 2654216 | tf_op jit(solution)/shard_map/ppermute | solution.py:188
  0.7 1.5 %copy-start = (bf16[1,576,1536]{2,1,0:T(8,128)(2,1)S(1)}, bf16[1,576,1536]{2,1,0:T(8,128)(2,1)}, u32[]{:S(2)}) copy-start(bf16[1,576,1536]{2,1,0:T(8,128)(2,1)} %param.7) | copy-start | bytes 5308420
  2.2 1.2 %copy-start.2 = (bf16[768,576]{0,1:T(8,128)(2,1)S(1)}, bf16[768,576]{0,1:T(8,128)(2,1)}, u32[]{:S(2)}) copy-start(bf16[768,576]{0,1:T(8,128)(2,1)} %param.5) | copy-start | bytes 2654212
  3.4 1.2 %copy-start.5 = (bf16[1,768,576]{1,2,0:T(8,128)(2,1)S(1)}, bf16[1,768,576]{1,2,0:T(8,128)(2,1)}, u32[]{:S(2)}) copy-start(bf16[1,768,576]{1,2,0:T(8,128)(2,1)} %param.8) | copy-start | bytes 2654212
  4.5 0.7 copy-start.6
  5.2 17.7 %copy-start.1 = (bf16[1,576,1536]{2,1,0:T(8,128)(2,1)S(1)}, bf16[1,576,1536]{2,1,0:T(8,128)(2,1)}, u32[]{:S(2)}) copy-start(bf16[1,576,1536]{2,1,0:T(8,128)(2,1)} %param.7) | copy-start | bytes 5308420
  9.2 13.7 %collective-permute-start = (bf16[576,768]{1,0:T(8,128)(2,1)S(1)}, bf16[576,768]{1,0:T(8,128)(2,1)S(1)}, u32[]{:S(2)}, u32[]{:S(2)}) collective-permute-start(bf16[576,768]{1,0:T(8,128)(2,1)S(1)} %get-tuple-element.33.next_ref), channel_id=1, source_target_pairs={{0,16},{16,32},{32,48},{48,64},{64,80},{80,96},{96,112},{112,128},... | collective-permute-start | bytes 2654216 | tf_op jit(solution)/shard_map/ppermute | solution.py:188
  26.7 7.5 %collective-permute-start.3 = (bf16[576,512]{1,0:T(8,128)(2,1)S(1)}, bf16[576,512]{1,0:T(8,128)(2,1)S(1)}, u32[]{:S(2)}, u32[]{:S(2)}) collective-permute-start(bf16[576,512]{1,0:T(8,128)(2,1)S(1)} %get-tuple-element.36._), channel_id=1, source_target_pairs={{0,240},{16,0},{32,16},{48,32},{64,48},{80,64},{96,80},{112,96},{1... | collective-permute-start | bytes 1769480 | tf_op jit(solution)/shard_map/ppermute | solution.py:188
  29.7 8.6 %collective-permute-start.2 = (bf16[576,256]{1,0:T(8,128)(2,1)S(1)}, bf16[576,256]{1,0:T(8,128)(2,1)S(1)}, u32[]{:S(2)}, u32[]{:S(2)}) collective-permute-start(bf16[576,256]{1,0:T(8,128)(2,1)S(1)} %get-tuple-element.37), channel_id=1, source_target_pairs={{0,240},{16,0},{32,16},{48,32},{64,48},{80,64},{96,80},{112,96},{1... | collective-permute-start | bytes 884744 | tf_op jit(solution)/shard_map/ppermute | solution.py:188
  30.5 3.7 %copy-start.3 = (bf16[768,576]{0,1:T(8,128)(2,1)S(1)}, bf16[768,576]{0,1:T(8,128)(2,1)}, u32[]{:S(2)}) copy-start(bf16[768,576]{0,1:T(8,128)(2,1)} %param.5) | copy-start | bytes 2654212
  34.2 4.1 %copy-start.7 = (f32[1,576]{1,0:T(1,128)S(1)}, f32[1,576]{1,0:T(1,128)}, u32[]{:S(2)}) copy-start(f32[1,576]{1,0:T(1,128)} %refs_8_.3) | copy-start | bytes 6916
  42.2 1.5 %copy-start.4 = (bf16[10608,128]{1,0:T(8,128)(2,1)}, bf16[10608,128]{1,0:T(8,128)(2,1)S(1)}, u32[]{:S(2)}) copy-start(bf16[10608,128]{1,0:T(8,128)(2,1)S(1)} %get-tuple-element.58) | copy-start | bytes 8146948
  43.8 44.1 %copy-start.8 = (u32[256]{0:T(256)S(1)}, u32[256]{0:T(256)}, u32[]{:S(2)}) copy-start(u32[256]{0:T(256)} %constant.43) | copy-start | bytes 3076
  84.6 4.5 %collective-permute-start.5 = (bf16[14,128]{1,0:T(8,128)(2,1)S(1)}, bf16[14,128]{1,0:T(8,128)(2,1)S(1)}, u32[]{:S(2)}, u32[]{:S(2)}) collective-permute-start(bf16[14,128]{1,0:T(8,128)(2,1)S(1)} %slice), channel_id=1, source_target_pairs={{0,1},{1,2},{2,3},{3,4},{4,5},{5,6},{6,7},{8,9},{9,10},{10,11},{11... | collective-permute-start | bytes 10760
  90.6 7.6 %collective-permute-start.4 = (bf16[656,128]{1,0:T(8,128)(2,1)S(1)}, bf16[656,128]{1,0:T(8,128)(2,1)S(1)}, u32[]{:S(2)}, u32[]{:S(2)}) collective-permute-start(bf16[656,128]{1,0:T(8,128)(2,1)S(1)} %get-tuple-element.62), channel_id=1, source_target_pairs={{0,8},{1,9},{2,10},{3,11},{4,12},{5,13},{6,14},{7,15},{8,0},{9,1},... | collective-permute-start | bytes 503816 | tf_op jit(solution)/shard_map/ppermute | solution.py:250

commit v4 on v3

--- a/solution.py
+++ b/solution.py
@@ -59,25 +59,40 @@
     return in_grad.astype(bf16), gain_term
 
 
-def forward_kernel(tok_ref, gu_ref, dn_t_ref, gain_ref, next_ref, normed_ref, act_ref, slope_ref, silu_ref, gu_t_ref, dn_ref):
+def forward_part(hidden, gain, gu_t_ref, dn_t_ref, next_ref, normed_ref, act_ref, slope_ref, silu_ref):
+    floated, inverse = norm_parts(hidden)
+    normed = (floated * inverse * gain).astype(bf16)
+    normed_ref[...] = normed
+    activated, slope, silu = project(normed, gu_t_ref[...])
+    act_ref[...] = activated
+    slope_ref[...] = slope.astype(bf16)
+    silu_ref[...] = silu.astype(bf16)
+    next_ref[...] = (floated + mul(dn_t_ref[...], activated)).astype(bf16)
+
+
+def first_kernel(span, *refs):
+    sources, held, (gu_t_ref, dn_ref), outs, sems = refs[:4], refs[4:8], refs[8:10], refs[10:15], refs[15]
+    copies = [pltpu.make_async_copy(src, dst, sems.at[i]) for i, (src, dst) in enumerate(zip(sources, held))]
+    for copy in copies:
+        copy.start()
+    gain_ref, tok_ref, gu_ref, dn_t_ref = held
+    copies[0].wait()
+    copies[1].wait()
+    copies[2].wait()
     gu_t_ref[...] = jnp.transpose(gu_ref[...])
+    copies[3].wait()
+    forward_part(tok_ref[:, span[0] : span[1]], column(gain_ref[...]), gu_t_ref, dn_t_ref, *outs)
     dn_ref[...] = jnp.transpose(dn_t_ref[...])
+
+
+def next_kernel(span, gain_ref, tok_ref, gu_t_ref, dn_t_ref, *outs):
+    forward_part(tok_ref[:, span[0] : span[1]], column(gain_ref[...]), gu_t_ref, dn_t_ref, *outs)
+
+
+def turn_kernel(h_ref, out_ref, gu_t_ref, gu_ref, dn_ref, gain_ref, _, in_ref, normed_ref, act_ref, mixed_ref, term_ref):
+    outgrad = out_ref[...]
     gain = column(gain_ref[...])
-    for lo, hi in SPANS:
-        floated, inverse = norm_parts(tok_ref[:, lo:hi])
-        normed = (floated * inverse * gain).astype(bf16)
-        normed_ref[:, lo:hi] = normed
-        activated, slope, silu = project(normed, gu_t_ref[...])
-        act_ref[:, lo:hi] = activated
-        slope_ref[:, lo:hi] = slope.astype(bf16)
-        silu_ref[:, lo:hi] = silu.astype(bf16)
-        next_ref[:, lo:hi] = (floated + mul(dn_t_ref[...], activated)).astype(bf16)
-
-
-def turn_kernel(span, h_ref, out_ref, gu_t_ref, gu_ref, dn_ref, gain_ref, _, in_ref, normed_ref, act_ref, mixed_ref, term_ref):
-    outgrad = out_ref[:, span[0] : span[1]]
-    gain = column(gain_ref[...])
-    floated, inverse = norm_parts(h_ref[:, span[0] : span[1]])
+    floated, inverse = norm_parts(h_ref[...])
     normed = (floated * inverse * gain).astype(bf16)
     normed_ref[...] = normed
     activated, slope, silu = project(normed, gu_t_ref[...])
@@ -89,12 +104,12 @@
     in_ref[...], term_ref[...] = back_through_norm(norm_grad, floated, inverse, outgrad, gain)
 
 
-def weight_kernel(out_ref, *refs):
+def weight_kernel(*refs):
     count = len(SPANS)
-    normed, mixed, acts, terms = [refs[i * count : (i + 1) * count] for i in range(4)]
-    gu_ref, dn_ref, gain_ref = refs[4 * count :]
+    outs, normed, mixed, acts, terms = [refs[i * count : (i + 1) * count] for i in range(5)]
+    gu_ref, dn_ref, gain_ref = refs[5 * count :]
     gu_ref[...] = functools.reduce(jnp.add, [mul_nt(a[...], b[...]) for a, b in zip(normed, mixed)])
-    dn_ref[...] = functools.reduce(jnp.add, [mul_nt(out_ref[:, lo:hi], a[...]) for (lo, hi), a in zip(SPANS, acts)])
+    dn_ref[...] = functools.reduce(jnp.add, [mul_nt(a[...], b[...]) for a, b in zip(outs, acts)])
     gain_ref[...] = functools.reduce(jnp.add, [t[...] for t in terms])
 
 
@@ -135,7 +150,6 @@
 
 def backward_kernel(span, last, *refs):
     tok_ref, out_ref, slope_ref, silu_ref, normed_ref, act_ref, dn_ref, gu_ref, gain_ref = refs[:9]
-    part = (slice(None), slice(*span))
     gu_sum_ref, dn_sum_ref, gain_sum_ref = refs[9:12]
     hid = dn_ref.shape[0]
     gain = column(gain_ref[...])
@@ -143,16 +157,16 @@
     act_grad = mul(dn_ref[...], outgrad)
     mixed = jnp.concatenate(
         [
-            (act_grad * slope_ref[part].astype(f32)).astype(bf16),
-            (act_grad * silu_ref[part].astype(f32)).astype(bf16),
+            (act_grad * slope_ref[...].astype(f32)).astype(bf16),
+            (act_grad * silu_ref[...].astype(f32)).astype(bf16),
         ],
         axis=0,
     )
-    floated, inverse = norm_parts(tok_ref[part])
+    floated, inverse = norm_parts(tok_ref[:, span[0] : span[1]])
     norm_grad = mul(gu_ref[...], mixed)
     in_grad, term = back_through_norm(norm_grad, floated, inverse, outgrad, gain)
-    gu_sum = gu_sum_ref[...] + mul_nt(normed_ref[part], mixed)
-    dn_sum = dn_sum_ref[...] + mul_nt(outgrad, act_ref[part])
+    gu_sum = gu_sum_ref[...] + mul_nt(normed_ref[...], mixed)
+    dn_sum = dn_sum_ref[...] + mul_nt(outgrad, act_ref[...])
     gain_sum = gain_sum_ref[...] + term
     if last:
         before_ref, grad_ref, total_ref, slots_ref, staged_ref, sems = refs[12:]
@@ -168,19 +182,20 @@
         gain_out[...] = gain_sum
 
 
-def call(kernel, outs, args, aliases={}, kept=True, scratch=(), free=0):
+def call(kernel, outs, args, flops, aliases={}, kept=True, scratch=(), free=0, moved=False):
     shaped = pltpu.VMEM if kept else jax.ShapeDtypeStruct
-    inside = pl.BlockSpec(memory_space=pltpu.VMEM)
+    inside, outside = pl.BlockSpec(memory_space=pltpu.VMEM), pl.BlockSpec(memory_space=pltpu.HBM)
     held = len(outs) - free
     return pl.pallas_call(
         kernel,
-        out_shape=[shaped(*o) for o in outs[:held]] + [jax.ShapeDtypeStruct(*o) for o in outs[held:]],
-        in_specs=[inside] * len(args),
-        out_specs=[inside] * held + [pl.BlockSpec(memory_space=pl.ANY)] * free,
+        out_shape=[shaped(*o) for o in outs[:held]] + [pltpu.HBM(*o) for o in outs[held:]],
+        in_specs=[outside if moved else inside] * len(args),
+        out_specs=[inside] * held + [outside] * free,
         input_output_aliases=aliases,
         scratch_shapes=scratch,
         compiler_params=pltpu.CompilerParams(vmem_limit_bytes=28 * 2**20),
-    )(*[pltpu.with_memory_space_constraint(a, pltpu.VMEM) for a in args])
+        cost_estimate=pl.CostEstimate(flops=flops, bytes_accessed=flops // 200, transcendentals=0),
+    )(*[pltpu.with_memory_space_constraint(a, pltpu.HBM if moved else pltpu.VMEM) for a in args])
 
 
 def passed_along(x, axis, by):
@@ -204,20 +219,37 @@
     width, rows = tok.shape
     hid = dn_t.shape[1]
     length = RING * SHORT
-    out = passed_along(cot, "blk", 1)
-    wide = [((n, rows), bf16) for n in (width, width, hid, hid, hid)]
-    nxt, normed, act, slope, silu, gu_t, dn = call(
-        forward_kernel, wide + [((2 * hid, width), bf16), ((hid, width), bf16)], (tok, gu, dn_t, gain)
-    )
-    hidden = passed_along(nxt, "blk", 1)
+    unit = 4 * width * hid
+    cots = [passed_along(cot[:, lo:hi], "blk", 1) for lo, hi in SPANS]
+    kept, nexts = [], []
+    for i, (lo, hi) in enumerate(SPANS):
+        shapes = [((n, hi - lo), bf16) for n in (width, width, hid, hid, hid)]
+        cost = 3 * unit * (hi - lo)
+        if i == 0:
+            args = (gain, tok, gu, dn_t)
+            held = [(a.shape, a.dtype) for a in args] + [((2 * hid, width), bf16), ((hid, width), bf16)]
+            gain, tok, gu, dn_t, gu_t, dn, *parts = call(
+                functools.partial(first_kernel, (lo, hi)),
+                held + shapes,
+                args,
+                cost,
+                scratch=[pltpu.SemaphoreType.DMA((len(args),))],
+                moved=True,
+            )
+        else:
+            parts = call(functools.partial(next_kernel, (lo, hi)), shapes, (gain, tok, gu_t, dn_t), cost)
+        nexts.append(parts[0])
+        kept.append(parts[1:])
+    hiddens = [passed_along(nxt, "blk", 1) for nxt in nexts]
     turned, returned = [], []
-    (after,) = call(touch_kernel, [((16, LANES), bf16)], (out, nxt))
-    for lo, hi in SPANS:
+    (after,) = call(touch_kernel, [((16, LANES), bf16)], (cots[0], nexts[-1]), unit)
+    for i, (lo, hi) in enumerate(SPANS):
         n = hi - lo
         in_grad, *parts = call(
-            functools.partial(turn_kernel, (lo, hi)),
+            turn_kernel,
             [((width, n), bf16)] * 2 + [((hid, n), bf16), ((2 * hid, n), bf16), ((width, LANES), f32)],
-            (hidden, out, gu_t, gu, dn, gain, after),
+            (hiddens[i], cots[i], gu_t, gu, dn, gain, after),
+            5 * unit * n,
         )
         after = in_grad
         turned.append(parts)
@@ -226,20 +258,21 @@
     sums = call(
         weight_kernel,
         sums_shape,
-        [out] + [part[i] for i in (0, 2, 1, 3) for part in turned],
+        cots + [part[i] for i in (0, 2, 1, 3) for part in turned],
+        3 * unit * rows,
     )
     before = None
-    for (lo, hi), back in zip(SPANS, returned):
+    for (lo, hi), back, (normed, act, slope, silu) in zip(SPANS, returned, kept):
         last = hi == rows
         args = (tok, back, slope, silu, normed, act, dn, gu, gain, *sums)
         kernel = functools.partial(backward_kernel, (lo, hi), last)
         if last:
             shapes = [((width, rows), bf16), ((length, LANES), bf16)]
             scratch = [pltpu.VMEM((length, LANES), f32), pltpu.VMEM((length, LANES), bf16), pltpu.SemaphoreType.DMA((RING,))]
-            grad, total = call(kernel, shapes, (*args, before), scratch=scratch, free=1)
+            grad, total = call(kernel, shapes, (*args, before), 6 * unit * (hi - lo), scratch=scratch, free=1)
         else:
             before, *sums = call(
-                kernel, [((width, hi - lo), bf16)] + sums_shape, args, {9: 1, 10: 2, 11: 3}
+                kernel, [((width, hi - lo), bf16)] + sums_shape, args, 6 * unit * (hi - lo), {9: 1, 10: 2, 11: 3}
             )
     rings = [[half * RING + place for place in range(RING)] for half in range(2)]
     share = lax.psum_scatter(total, "rep", scatter_dimension=0, axis_index_groups=rings, tiled=True)
@@ -253,6 +286,7 @@
         split_kernel,
         [((SHARE, 1, 2 * hid), f32), ((SHARE, 1, hid), f32), ((1, SHARE), f32)],
         (mine, theirs),
+        unit,
         kept=False,
     )
     return grad.T, gu_mine.transpose(1, 0, 2), dn_mine.transpose(1, 2, 0), gain_mine

time: 99.4 us -> 93.6 us (0.942)
  waiting for transfers between devices: 19.8 us -> 13.3 us
  local copies, waits for them, and re-layouts: 9.03 us -> 5.1 us
  Pallas kernels: 21.8 us -> 25.1 us
    ppermute x4 -> x6, waiting for transfers between devices: 13.7 us -> 7.33 us  [passed_along(): return lax.ppermute(x, axis, [(i, (i + by) % peers) for i in range(peers)])]
    unnamed x23 -> x7, local copies, waits for them, and re-layouts: 8.92 us -> 2.91 us
    pallas_call x8 -> x9, Pallas kernels: 21.8 us -> 25.1 us  [call(): pl.pallas_call(kernel, out_shape=[shaped(*o) for o in outs[:held]] + [plt...]
    slice x0 -> x2, local copies, waits for them, and re-layouts: none -> 2.09 us  [per_device(): cots = [passed_along(cot[:, lo:hi], 'blk', 1) for lo, hi in SPANS]]
    ppermute x4 -> x6, starting transfers between devices: 2.43 us -> 3.01 us  [passed_along(): return lax.ppermute(x, axis, [(i, (i + by) % peers) for i in range(peers)])]
  transfers between devices with their start and end apart: 6 -> 8, of which waited for: 4 -> 3; matrix products, arithmetic and copies ran while one was open for 2% -> 3% of each run, Pallas kernels for 13% -> 22%
where the time goes in v4:
time: 93.6 us; the launch traced here: 92.4 us
  blocking collectives  40.8 us (44%)
  Pallas kernels  25.1 us (27%)
  waiting for transfers between devices  13.3 us (14%)
  starting transfers between devices  6.53 us (7%)
  local copies, waits for them, and re-layouts  5.1 us (5%)
  between operations  1.49 us (2%)
    unnamed x1, blocking collectives  40.8 us
    pallas_call x9, Pallas kernels, call(): pl.pallas_call(kernel, out_shape=[shaped(*o) for o in outs[:held]] + [plt...  25.1 us
    ppermute x6, waiting for transfers between devices, passed_along(): return lax.ppermute(x, axis, [(i, (i + by) % peers) for i in range(peers)])  7.33 us
    ppermute x1, waiting for transfers between devices, per_device(): lax.ppermute(theirs, 'rep', [(i, (i + RING) % (2 * RING)) for i in range(...  5.96 us
    ppermute x6, starting transfers between devices, passed_along(): return lax.ppermute(x, axis, [(i, (i + by) % peers) for i in range(peers)])  3.01 us
    unnamed x1, starting transfers between devices  2.94 us
    unnamed x7, local copies, waits for them, and re-layouts  2.91 us
    slice x2, local copies, waits for them, and re-layouts, per_device(): cots = [passed_along(cot[:, lo:hi], 'blk', 1) for lo, hi in SPANS]  2.09 us
  transfers between devices with their start and end apart: 8, of which 3 were waited for; matrix products, arithmetic and copies ran while one was open for 3% of the time, Pallas kernels for 22%

profile of v4, /device:TPU:20, one launch (start us, length us, event | category | flops | bytes accessed | tf_op | source)
XLA Modules:
  0.0 92.4 jit_solution(15531259753957584308)
XLA Ops:
  0.6 1.1 %slice.9 = bf16[576,512]{1,0:T(8,128)(2,1)S(1)} slice(bf16[576,768]{1,0:T(8,128)(2,1)} %bitcast.13), slice={[0:576], [0:512]} | slice | bytes 1179648 | tf_op jit(solution)/shard_map/slice | solution.py:223
  1.7 0.1 collective-permute-start.3
  1.8 5.0 %shard_map.84 = (f32[1,576]{1,0:T(1,128)S(1)}, bf16[576,768]{1,0:T(8,128)(2,1)S(1)}, bf16[576,1536]{1,0:T(8,128)(2,1)S(1)}, bf16[576,768]{1,0:T(8,128)(2,1)S(1)}...) custom-call(f32[1,576]{1,0:T(1,128)} %refs_0_.1, ...), custom_call_target="tpu_custom_call" | custom-call | flops 2717908992 | bytes 13589544 | tf_op jit(solution)/shard_map/pallas_call | solution.py:189
  6.8 1.5 %collective-permute-start.2 = (bf16[576,512]{1,0:T(8,128)(2,1)S(1)}, bf16[576,512]{1,0:T(8,128)(2,1)S(1)}, u32[]{:S(2)}, u32[]{:S(2)}) collective-permute-start(bf16[576,512]{1,0:T(8,128)(2,1)S(1)} %get-tuple-element.49), channel_id=1, source_target_pairs={{0,16},{16,32},{32,48},{48,64},{64,80},{80,96},{96,112},{112,128},... | collective-permute-start | bytes 1769480 | tf_op jit(solution)/shard_map/ppermute | solution.py:203
  8.3 1.9 %shard_map.85 = (bf16[576,256]{1,0:T(8,128)(2,1)S(1)}, bf16[576,256]{1,0:T(8,128)(2,1)S(1)}, bf16[768,256]{1,0:T(8,128)(2,1)S(1)}, bf16[768,256]{1,0:T(8,128)(2,1)S(1)}, bf16[768,256]{1,0:T(8,128)(2,1)S(1)}) custom-call(f32[1,576]{1,0:T(1,128)S(1)} %get-tuple-element.43.gain_ref.refs_8_, bf16[576,768]{1,0:T(8,128)(2,1)S(1)} %get-tuple-element.42.tok_ref.refs_0_, ...), custom_call_target="tpu_custom_call" | custom-call | flops 1358954496 | bytes 6794772 | tf_op jit(solution)/shard_map/pallas_call | solution.py:189
  10.1 0.1 collective-permute-start
  10.2 1.0 %slice.8 = bf16[576,256]{1,0:T(8,128)(2,1)S(1)} slice(bf16[576,768]{1,0:T(8,128)(2,1)} %bitcast.14), slice={[0:576], [512:768]} | slice | bytes 589824 | tf_op jit(solution)/shard_map/slice | solution.py:223
  11.2 1.0 %collective-permute-start.1 = (bf16[576,256]{1,0:T(8,128)(2,1)S(1)}, bf16[576,256]{1,0:T(8,128)(2,1)S(1)}, u32[]{:S(2)}, u32[]{:S(2)}) collective-permute-start(bf16[576,256]{1,0:T(8,128)(2,1)S(1)} %slice.8), channel_id=1, source_target_pairs={{0,16},{16,32},{32,48},{48,64},{64,80},{80,96},{96,112},{112,128},... | collective-permute-start | bytes 884744 | tf_op jit(solution)/shard_map/ppermute | solution.py:203
  12.3 0.0 collective-permute-done.3.out_ref.refs_0_
  12.3 5.2 %collective-permute-done.2.h_ref = bf16[576,512]{1,0:T(8,128)(2,1)S(1)} collective-permute-done((bf16[576,512]{1,0:T(8,128)(2,1)S(1)}, bf16[576,512]{1,0:T(8,128)(2,1)S(1)}, u32[]{:S(2)}, u32[]{:S(2)}) %collective-permute-start.2) | collective-permute-done | bytes 589856 | tf_op jit(solution)/shard_map/ppermute | solution.py:203
  17.4 3.9 %shard_map.87 = (bf16[576,512]{1,0:T(8,128)(2,1)S(1)}, bf16[576,512]{1,0:T(8,128)(2,1)S(1)}, bf16[768,512]{1,0:T(8,128)(2,1)S(1)}, bf16[1536,512]{1,0:T(8,128)(2,1)S(1)}, f32[576,128]{1,0:T(8,128)S(1)}) custom-call(bf16[576,512]{1,0:T(8,128)(2,1)S(1)} %collective-permute-done.2.h_ref, bf16[576,512]{1,0:T(8,128)(2,1)S(1)} %collective-permute-done.3.out_ref.refs_0_, ...), custom_call_target="tpu_custom_call" | custom-call | flops 4529848320 | bytes 22649240 | tf_op jit(solution)/shard_map/pallas_call | solution.py:189
  21.3 0.3 collective-permute-start.5
  21.6 0.0 collective-permute-done.h_ref
  21.6 2.1 %collective-permute-done.1.out_ref.refs_1_ = bf16[576,256]{1,0:T(8,128)(2,1)S(1)} collective-permute-done((bf16[576,256]{1,0:T(8,128)(2,1)S(1)}, bf16[576,256]{1,0:T(8,128)(2,1)S(1)}, u32[]{:S(2)}, u32[]{:S(2)}) %collective-permute-start.1) | collective-permute-done | bytes 294944 | tf_op jit(solution)/shard_map/ppermute | solution.py:203
  23.8 2.9 %shard_map.88 = (bf16[576,256]{1,0:T(8,128)(2,1)S(1)}, bf16[576,256]{1,0:T(8,128)(2,1)S(1)}, bf16[768,256]{1,0:T(8,128)(2,1)S(1)}, bf16[1536,256]{1,0:T(8,128)(2,1)S(1)}, f32[576,128]{1,0:T(8,128)S(1)}) custom-call(bf16[576,256]{1,0:T(8,128)(2,1)S(1)} %collective-permute-done.h_ref, bf16[576,256]{1,0:T(8,128)(2,1)S(1)} %collective-permute-done.1.out_ref.refs_1_, ...), custom_call_target="tpu_custom_call" | custom-call | flops 2264924160 | bytes 11324620 | tf_op jit(solution)/shard_map/pallas_call | solution.py:189
  26.7 0.1 collective-permute-start.4
  26.8 2.3 %shard_map.89 = (f32[576,1536]{1,0:T(8,128)S(1)}, f32[576,768]{1,0:T(8,128)S(1)}, f32[576,128]{1,0:T(8,128)S(1)}) custom-call(bf16[576,512]{1,0:T(8,128)(2,1)S(1)} %collective-permute-done.3.out_ref.refs_0_, bf16[576,256]{1,0:T(8,128)(2,1)S(1)} %collective-permute-done.1.out_ref.refs_1_, bf16[576,512]{1,0:T(8,128)(2,1)S(1)} %get-tuple-element.60.refs_2_, ...), custom_call_target="tpu_custom_call" | custom-call | flops 4076863488 | bytes 20384316 | tf_op jit(solution)/shard_map/pallas_call | solution.py:189
  29.1 0.0 collective-permute-done.5.refs_1_
  29.1 4.2 %shard_map.90 = (bf16[576,512]{1,0:T(8,128)(2,1)S(1)}, f32[576,1536]{1,0:T(8,128)S(1)}, f32[576,768]{1,0:T(8,128)S(1)}, f32[576,128]{1,0:T(8,128)S(1)}) custom-call(bf16[576,768]{1,0:T(8,128)(2,1)S(1)} %get-tuple-element.42.tok_ref.refs_0_, ...), custom_call_target="tpu_custom_call", output_to_operand_aliasing={{1}: (9, {}), {2}: (10, {}), {3}: (11, {})} | custom-call | flops 5435817984 | bytes 27179088 | tf_op jit(solution)/shard_map/pallas_call | solution.py:189
  33.3 0.0 collective-permute-done.4.refs_1_
  33.3 4.0 %shard_map.91 = (bf16[576,768]{1,0:T(8,128)(2,1)S(1)}, bf16[10608,128]{1,0:T(8,128)(2,1)}) custom-call(bf16[576,768]{1,0:T(8,128)(2,1)S(1)} %get-tuple-element.42.tok_ref.refs_0_, bf16[576,256]{1,0:T(8,128)(2,1)S(1)} %collective-permute-done.4.refs_1_, bf16[768,256]{1,0:T(8,128)(2,1)S(1)} %get-tuple-element.52.refs_2_, ...), custom_call_target="tpu_custom_call" | custom-call | flops 2717908992 | bytes 13589544 | tf_op jit(solution)/shard_map/pallas_call | solution.py:189
  37.4 0.0 copy-start
  37.4 40.8 %fusion = bf16[1328,128]{1,0:T(8,128)(2,1)S(1)} fusion(bf16[10608,128]{1,0:T(8,128)(2,1)} %get-tuple-element.76), kind=kCustom, calls=%all-reduce-scatter | all-reduce-scatter fusion | flops 1359873 | bytes 3056640
  78.2 2.9 %collective-permute-start.7 = (bf16[14,128]{1,0:T(8,128)(2,1)S(1)}, bf16[14,128]{1,0:T(8,128)(2,1)S(1)}, u32[]{:S(2)}, u32[]{:S(2)}) collective-permute-start(bf16[14,128]{1,0:T(8,128)(2,1)S(1)} %slice.10), channel_id=1, source_target_pairs={{0,1},{1,2},{2,3},{3,4},{4,5},{5,6},{6,7},{8,9},{9,10},{10,11},{11... | collective-permute-start | bytes 10760
  81.2 0.0 copy-done
  81.2 0.6 dynamic-slice.4
  82.5 0.0 collective-permute-done.7
  82.5 1.3 %concatenate = bf16[1342,128]{1,0:T(8,128)(2,1)S(1)} concatenate(bf16[14,128]{1,0:T(8,128)(2,1)S(1)} %collective-permute-done.7, bf16[1328,128]{1,0:T(8,128)(2,1)S(1)} %fusion), dimensions={0} | concatenate | bytes 687104
  83.8 0.1 constant_dynamic-slice_fusion
  83.9 0.1 constant_dynamic-slice_fusion.1
  84.0 0.6 collective-permute-start.6
  84.6 0.9 copy.15
  85.5 6.0 %collective-permute-done.6.other_ref = bf16[656,128]{1,0:T(8,128)(2,1)S(1)} collective-permute-done((bf16[656,128]{1,0:T(8,128)(2,1)S(1)}, bf16[656,128]{1,0:T(8,128)(2,1)S(1)}, u32[]{:S(2)}, u32[]{:S(2)}) %collective-permute-start.6) | collective-permute-done | bytes 167968 | tf_op jit(solution)/shard_map/ppermute | solution.py:283
  91.5 0.9 shard_map.92
  (2 shorter events, 0.0 us)
Async XLA Ops:
  1.7 10.5 %collective-permute-start.3 = (bf16[576,512]{1,0:T(8,128)(2,1)S(1)}, bf16[576,512]{1,0:T(8,128)(2,1)S(1)}, u32[]{:S(2)}, u32[]{:S(2)}) collective-permute-start(bf16[576,512]{1,0:T(8,128)(2,1)S(1)} %slice.9), channel_id=1, source_target_pairs={{0,16},{16,32},{32,48},{48,64},{64,80},{80,96},{96,112},{112,128},... | collective-permute-start | bytes 1769480 | tf_op jit(solution)/shard_map/ppermute | solution.py:203
  6.8 10.6 %collective-permute-start.2 = (bf16[576,512]{1,0:T(8,128)(2,1)S(1)}, bf16[576,512]{1,0:T(8,128)(2,1)S(1)}, u32[]{:S(2)}, u32[]{:S(2)}) collective-permute-start(bf16[576,512]{1,0:T(8,128)(2,1)S(1)} %get-tuple-element.49), channel_id=1, source_target_pairs={{0,16},{16,32},{32,48},{48,64},{64,80},{80,96},{96,112},{112,128},... | collective-permute-start | bytes 1769480 | tf_op jit(solution)/shard_map/ppermute | solution.py:203
  10.1 11.5 %collective-permute-start = (bf16[576,256]{1,0:T(8,128)(2,1)S(1)}, bf16[576,256]{1,0:T(8,128)(2,1)S(1)}, u32[]{:S(2)}, u32[]{:S(2)}) collective-permute-start(bf16[576,256]{1,0:T(8,128)(2,1)S(1)} %get-tuple-element.46.next_ref), channel_id=1, source_target_pairs={{0,16},{16,32},{32,48},{48,64},{64,80},{80,96},{96,112},{112,128},... | collective-permute-start | bytes 884744 | tf_op jit(solution)/shard_map/ppermute | solution.py:203
  11.2 12.5 %collective-permute-start.1 = (bf16[576,256]{1,0:T(8,128)(2,1)S(1)}, bf16[576,256]{1,0:T(8,128)(2,1)S(1)}, u32[]{:S(2)}, u32[]{:S(2)}) collective-permute-start(bf16[576,256]{1,0:T(8,128)(2,1)S(1)} %slice.8), channel_id=1, source_target_pairs={{0,16},{16,32},{32,48},{48,64},{64,80},{80,96},{96,112},{112,128},... | collective-permute-start | bytes 884744 | tf_op jit(solution)/shard_map/ppermute | solution.py:203
  21.3 7.8 %collective-permute-start.5 = (bf16[576,512]{1,0:T(8,128)(2,1)S(1)}, bf16[576,512]{1,0:T(8,128)(2,1)S(1)}, u32[]{:S(2)}, u32[]{:S(2)}) collective-permute-start(bf16[576,512]{1,0:T(8,128)(2,1)S(1)} %get-tuple-element.50._), channel_id=1, source_target_pairs={{0,240},{16,0},{32,16},{48,32},{64,48},{80,64},{96,80},{112,96},{1... | collective-permute-start | bytes 1769480 | tf_op jit(solution)/shard_map/ppermute | solution.py:203
  26.7 6.6 %collective-permute-start.4 = (bf16[576,256]{1,0:T(8,128)(2,1)S(1)}, bf16[576,256]{1,0:T(8,128)(2,1)S(1)}, u32[]{:S(2)}, u32[]{:S(2)}) collective-permute-start(bf16[576,256]{1,0:T(8,128)(2,1)S(1)} %get-tuple-element.51), channel_id=1, source_target_pairs={{0,240},{16,0},{32,16},{48,32},{64,48},{80,64},{96,80},{112,96},{1... | collective-permute-start | bytes 884744 | tf_op jit(solution)/shard_map/ppermute | solution.py:203
  37.4 43.8 %copy-start = (u32[256]{0:T(256)S(1)}, u32[256]{0:T(256)}, u32[]{:S(2)}) copy-start(u32[256]{0:T(256)} %constant.43) | copy-start | bytes 3076
  78.2 4.3 %collective-permute-start.7 = (bf16[14,128]{1,0:T(8,128)(2,1)S(1)}, bf16[14,128]{1,0:T(8,128)(2,1)S(1)}, u32[]{:S(2)}, u32[]{:S(2)}) collective-permute-start(bf16[14,128]{1,0:T(8,128)(2,1)S(1)} %slice.10), channel_id=1, source_target_pairs={{0,1},{1,2},{2,3},{3,4},{4,5},{5,6},{6,7},{8,9},{9,10},{10,11},{11... | collective-permute-start | bytes 10760
  84.0 7.5 %collective-permute-start.6 = (bf16[656,128]{1,0:T(8,128)(2,1)S(1)}, bf16[656,128]{1,0:T(8,128)(2,1)S(1)}, u32[]{:S(2)}, u32[]{:S(2)}) collective-permute-start(bf16[656,128]{1,0:T(8,128)(2,1)S(1)} %get-tuple-element.80), channel_id=1, source_target_pairs={{0,8},{1,9},{2,10},{3,11},{4,12},{5,13},{6,14},{7,15},{8,0},{9,1},... | collective-permute-start | bytes 503816 | tf_op jit(solution)/shard_map/ppermute | solution.py:283

commit v5 on v4

--- a/solution.py
+++ b/solution.py
@@ -104,13 +104,12 @@
     in_ref[...], term_ref[...] = back_through_norm(norm_grad, floated, inverse, outgrad, gain)
 
 
-def weight_kernel(*refs):
-    count = len(SPANS)
-    outs, normed, mixed, acts, terms = [refs[i * count : (i + 1) * count] for i in range(5)]
-    gu_ref, dn_ref, gain_ref = refs[5 * count :]
-    gu_ref[...] = functools.reduce(jnp.add, [mul_nt(a[...], b[...]) for a, b in zip(normed, mixed)])
-    dn_ref[...] = functools.reduce(jnp.add, [mul_nt(a[...], b[...]) for a, b in zip(outs, acts)])
-    gain_ref[...] = functools.reduce(jnp.add, [t[...] for t in terms])
+def weight_kernel(out_ref, normed_ref, mixed_ref, act_ref, term_ref, *refs):
+    before, (gu_ref, dn_ref, gain_ref) = refs[:-3], refs[-3:]
+    sums = [mul_nt(normed_ref[...], mixed_ref[...]), mul_nt(out_ref[...], act_ref[...]), term_ref[...]]
+    if before:
+        sums = [ref[...] + x for ref, x in zip(before, sums)]
+    gu_ref[...], dn_ref[...], gain_ref[...] = sums
 
 
 def fill_slots(slots_ref, staged_ref, total_ref, sems, gu_sum, dn_sum, gain_sum):
@@ -241,26 +240,21 @@
         nexts.append(parts[0])
         kept.append(parts[1:])
     hiddens = [passed_along(nxt, "blk", 1) for nxt in nexts]
-    turned, returned = [], []
+    sums_shape = [((width, 2 * hid), f32), ((width, hid), f32), ((width, LANES), f32)]
+    sums, returned = [], []
     (after,) = call(touch_kernel, [((16, LANES), bf16)], (cots[0], nexts[-1]), unit)
     for i, (lo, hi) in enumerate(SPANS):
         n = hi - lo
-        in_grad, *parts = call(
+        in_grad, normed, act, mixed, term = call(
             turn_kernel,
             [((width, n), bf16)] * 2 + [((hid, n), bf16), ((2 * hid, n), bf16), ((width, LANES), f32)],
             (hiddens[i], cots[i], gu_t, gu, dn, gain, after),
             5 * unit * n,
         )
-        after = in_grad
-        turned.append(parts)
+        args = (cots[i], normed, mixed, act, term, *sums)
+        sums = call(weight_kernel, sums_shape, args, 3 * unit * n, {5: 0, 6: 1, 7: 2} if sums else {})
+        after = sums[-1]
         returned.append(passed_along(in_grad, "blk", -1))
-    sums_shape = [((width, 2 * hid), f32), ((width, hid), f32), ((width, LANES), f32)]
-    sums = call(
-        weight_kernel,
-        sums_shape,
-        cots + [part[i] for i in (0, 2, 1, 3) for part in turned],
-        3 * unit * rows,
-    )
     before = None
     for (lo, hi), back, (normed, act, slope, silu) in zip(SPANS, returned, kept):
         last = hi == rows

time: 93.6 us -> 92.8 us (level); the launches traced: 92.4 us -> 92.5 us
    pallas_call x9 -> x10, Pallas kernels: 25.1 us -> 25.4 us  [call(): pl.pallas_call(kernel, out_shape=[shaped(*o) for o in outs[:held]] + [plt...]
  transfers between devices with their start and end apart: 8 -> 8, of which waited for: 3 -> 4; matrix products, arithmetic and copies ran while one was open for 3% -> 3% of each run, Pallas kernels for 22% -> 22%
where the time goes in v5:
time: 92.8 us; the launch traced here: 92.5 us
  blocking collectives  40.7 us (44%)
  Pallas kernels  25.4 us (27%)
  waiting for transfers between devices  13 us (14%)
  starting transfers between devices  6.77 us (7%)
  local copies, waits for them, and re-layouts  5.1 us (5%)
  between operations  1.49 us (2%)
    unnamed x1, blocking collectives  40.7 us
    pallas_call x10, Pallas kernels, call(): pl.pallas_call(kernel, out_shape=[shaped(*o) for o in outs[:held]] + [plt...  25.4 us
    ppermute x6, waiting for transfers between devices, passed_along(): return lax.ppermute(x, axis, [(i, (i + by) % peers) for i in range(peers)])  6.93 us
    ppermute x1, waiting for transfers between devices, per_device(): lax.ppermute(theirs, 'rep', [(i, (i + RING) % (2 * RING)) for i in range(...  6.09 us
    unnamed x1, starting transfers between devices  3.17 us
    ppermute x6, starting transfers between devices, passed_along(): return lax.ppermute(x, axis, [(i, (i + by) % peers) for i in range(peers)])  3.01 us
    unnamed x7, local copies, waits for them, and re-layouts  2.91 us
    slice x2, local copies, waits for them, and re-layouts, per_device(): cots = [passed_along(cot[:, lo:hi], 'blk', 1) for lo, hi in SPANS]  2.09 us
  transfers between devices with their start and end apart: 8, of which 4 were waited for; matrix products, arithmetic and copies ran while one was open for 3% of the time, Pallas kernels for 22%

profile of v5, /device:TPU:20, one launch (start us, length us, event | category | flops | bytes accessed | tf_op | source)
XLA Modules:
  0.0 92.5 jit_solution(2290619343271097722)
XLA Ops:
  0.6 1.1 %slice.9 = bf16[576,512]{1,0:T(8,128)(2,1)S(1)} slice(bf16[576,768]{1,0:T(8,128)(2,1)} %bitcast.13), slice={[0:576], [0:512]} | slice | bytes 1179648 | tf_op jit(solution)/shard_map/slice | solution.py:222
  1.7 0.1 collective-permute-start.2
  1.8 5.0 %shard_map.84 = (f32[1,576]{1,0:T(1,128)S(1)}, bf16[576,768]{1,0:T(8,128)(2,1)S(1)}, bf16[576,1536]{1,0:T(8,128)(2,1)S(1)}, bf16[576,768]{1,0:T(8,128)(2,1)S(1)}...) custom-call(f32[1,576]{1,0:T(1,128)} %refs_0_.1, ...), custom_call_target="tpu_custom_call" | custom-call | flops 2717908992 | bytes 13589544 | tf_op jit(solution)/shard_map/pallas_call | solution.py:188
  6.8 1.5 %collective-permute-start.3 = (bf16[576,512]{1,0:T(8,128)(2,1)S(1)}, bf16[576,512]{1,0:T(8,128)(2,1)S(1)}, u32[]{:S(2)}, u32[]{:S(2)}) collective-permute-start(bf16[576,512]{1,0:T(8,128)(2,1)S(1)} %get-tuple-element.52), channel_id=1, source_target_pairs={{0,16},{16,32},{32,48},{48,64},{64,80},{80,96},{96,112},{112,128},... | collective-permute-start | bytes 1769480 | tf_op jit(solution)/shard_map/ppermute | solution.py:202
  8.3 1.9 %shard_map.85 = (bf16[576,256]{1,0:T(8,128)(2,1)S(1)}, bf16[576,256]{1,0:T(8,128)(2,1)S(1)}, bf16[768,256]{1,0:T(8,128)(2,1)S(1)}, bf16[768,256]{1,0:T(8,128)(2,1)S(1)}, bf16[768,256]{1,0:T(8,128)(2,1)S(1)}) custom-call(f32[1,576]{1,0:T(1,128)S(1)} %get-tuple-element.46.gain_ref.refs_8_, bf16[576,768]{1,0:T(8,128)(2,1)S(1)} %get-tuple-element.45.tok_ref.refs_0_, ...), custom_call_target="tpu_custom_call" | custom-call | flops 1358954496 | bytes 6794772 | tf_op jit(solution)/shard_map/pallas_call | solution.py:188
  10.1 0.1 collective-permute-start
  10.2 1.0 %slice.8 = bf16[576,256]{1,0:T(8,128)(2,1)S(1)} slice(bf16[576,768]{1,0:T(8,128)(2,1)} %bitcast.14), slice={[0:576], [512:768]} | slice | bytes 589824 | tf_op jit(solution)/shard_map/slice | solution.py:222
  11.2 1.0 %collective-permute-start.1 = (bf16[576,256]{1,0:T(8,128)(2,1)S(1)}, bf16[576,256]{1,0:T(8,128)(2,1)S(1)}, u32[]{:S(2)}, u32[]{:S(2)}) collective-permute-start(bf16[576,256]{1,0:T(8,128)(2,1)S(1)} %slice.8), channel_id=1, source_target_pairs={{0,16},{16,32},{32,48},{48,64},{64,80},{80,96},{96,112},{112,128},... | collective-permute-start | bytes 884744 | tf_op jit(solution)/shard_map/ppermute | solution.py:202
  12.3 0.0 collective-permute-done.2.out_ref
  12.3 5.2 %collective-permute-done.3.h_ref = bf16[576,512]{1,0:T(8,128)(2,1)S(1)} collective-permute-done((bf16[576,512]{1,0:T(8,128)(2,1)S(1)}, bf16[576,512]{1,0:T(8,128)(2,1)S(1)}, u32[]{:S(2)}, u32[]{:S(2)}) %collective-permute-start.3) | collective-permute-done | bytes 589856 | tf_op jit(solution)/shard_map/ppermute | solution.py:202
  17.4 3.9 %shard_map.87 = (bf16[576,512]{1,0:T(8,128)(2,1)S(1)}, bf16[576,512]{1,0:T(8,128)(2,1)S(1)}, bf16[768,512]{1,0:T(8,128)(2,1)S(1)}, bf16[1536,512]{1,0:T(8,128)(2,1)S(1)}, f32[576,128]{1,0:T(8,128)S(1)}) custom-call(bf16[576,512]{1,0:T(8,128)(2,1)S(1)} %collective-permute-done.3.h_ref, bf16[576,512]{1,0:T(8,128)(2,1)S(1)} %collective-permute-done.2.out_ref, ...), custom_call_target="tpu_custom_call" | custom-call | flops 4529848320 | bytes 22649240 | tf_op jit(solution)/shard_map/pallas_call | solution.py:188
  21.3 0.3 collective-permute-start.5
  21.6 1.6 %shard_map.88 = (f32[576,1536]{1,0:T(8,128)S(1)}, f32[576,768]{1,0:T(8,128)S(1)}, f32[576,128]{1,0:T(8,128)S(1)}) custom-call(bf16[576,512]{1,0:T(8,128)(2,1)S(1)} %collective-permute-done.2.out_ref, bf16[576,512]{1,0:T(8,128)(2,1)S(1)} %get-tuple-element.53.normed_ref, bf16[1536,512]{1,0:T(8,128)(2,1)S(1)} %get-tuple-element.54.mixed_ref, ...), custom_call_target="tpu_custom_call" | custom-call | flops 2717908992 | bytes 13589544 | tf_op jit(solution)/shard_map/pallas_call | solution.py:188
  23.2 0.0 collective-permute-done.h_ref
  23.2 0.6 collective-permute-done.1.out_ref
  23.8 2.9 %shard_map.89 = (bf16[576,256]{1,0:T(8,128)(2,1)S(1)}, bf16[576,256]{1,0:T(8,128)(2,1)S(1)}, bf16[768,256]{1,0:T(8,128)(2,1)S(1)}, bf16[1536,256]{1,0:T(8,128)(2,1)S(1)}, f32[576,128]{1,0:T(8,128)S(1)}) custom-call(bf16[576,256]{1,0:T(8,128)(2,1)S(1)} %collective-permute-done.h_ref, bf16[576,256]{1,0:T(8,128)(2,1)S(1)} %collective-permute-done.1.out_ref, ...), custom_call_target="tpu_custom_call" | custom-call | flops 2264924160 | bytes 11324620 | tf_op jit(solution)/shard_map/pallas_call | solution.py:188
  26.7 0.1 collective-permute-start.4
  26.8 1.0 %shard_map.90 = (f32[576,1536]{1,0:T(8,128)S(1)}, f32[576,768]{1,0:T(8,128)S(1)}, f32[576,128]{1,0:T(8,128)S(1)}) custom-call(bf16[576,256]{1,0:T(8,128)(2,1)S(1)} %collective-permute-done.1.out_ref, bf16[576,256]{1,0:T(8,128)(2,1)S(1)} %get-tuple-element.68.normed_ref, ...), custom_call_target="tpu_custom_call", output_to_operand_aliasing={{0}: (5, {}), {1}: (6, {}), {2}: (7, {})} | custom-call | flops 1358954496 | bytes 6794772 | tf_op jit(solution)/shard_map/pallas_call | solution.py:188
  27.8 1.2 %collective-permute-done.5.refs_1_ = bf16[576,512]{1,0:T(8,128)(2,1)S(1)} collective-permute-done((bf16[576,512]{1,0:T(8,128)(2,1)S(1)}, bf16[576,512]{1,0:T(8,128)(2,1)S(1)}, u32[]{:S(2)}, u32[]{:S(2)}) %collective-permute-start.5) | collective-permute-done | bytes 589856 | tf_op jit(solution)/shard_map/ppermute | solution.py:202
  29.0 4.2 %shard_map.91 = (bf16[576,512]{1,0:T(8,128)(2,1)S(1)}, f32[576,1536]{1,0:T(8,128)S(1)}, f32[576,768]{1,0:T(8,128)S(1)}, f32[576,128]{1,0:T(8,128)S(1)}) custom-call(bf16[576,768]{1,0:T(8,128)(2,1)S(1)} %get-tuple-element.45.tok_ref.refs_0_, ...), custom_call_target="tpu_custom_call", output_to_operand_aliasing={{1}: (9, {}), {2}: (10, {}), {3}: (11, {})} | custom-call | flops 5435817984 | bytes 27179088 | tf_op jit(solution)/shard_map/pallas_call | solution.py:188
  33.2 0.0 collective-permute-done.4.refs_1_
  33.2 4.1 %shard_map.92 = (bf16[576,768]{1,0:T(8,128)(2,1)S(1)}, bf16[10608,128]{1,0:T(8,128)(2,1)}) custom-call(bf16[576,768]{1,0:T(8,128)(2,1)S(1)} %get-tuple-element.45.tok_ref.refs_0_, bf16[576,256]{1,0:T(8,128)(2,1)S(1)} %collective-permute-done.4.refs_1_, bf16[768,256]{1,0:T(8,128)(2,1)S(1)} %get-tuple-element.59.refs_2_, ...), custom_call_target="tpu_custom_call" | custom-call | flops 2717908992 | bytes 13589544 | tf_op jit(solution)/shard_map/pallas_call | solution.py:188
  37.3 0.0 copy-start
  37.3 40.7 %fusion = bf16[1328,128]{1,0:T(8,128)(2,1)S(1)} fusion(bf16[10608,128]{1,0:T(8,128)(2,1)} %get-tuple-element.82), kind=kCustom, calls=%all-reduce-scatter | all-reduce-scatter fusion | flops 1359873 | bytes 3056640
  78.0 3.2 %collective-permute-start.7 = (bf16[14,128]{1,0:T(8,128)(2,1)S(1)}, bf16[14,128]{1,0:T(8,128)(2,1)S(1)}, u32[]{:S(2)}, u32[]{:S(2)}) collective-permute-start(bf16[14,128]{1,0:T(8,128)(2,1)S(1)} %slice.10), channel_id=1, source_target_pairs={{0,1},{1,2},{2,3},{3,4},{4,5},{5,6},{6,7},{8,9},{9,10},{10,11},{11... | collective-permute-start | bytes 10760
  81.2 0.0 copy-done
  81.2 0.6 dynamic-slice.4
  82.5 0.0 collective-permute-done.7
  82.5 1.3 %concatenate = bf16[1342,128]{1,0:T(8,128)(2,1)S(1)} concatenate(bf16[14,128]{1,0:T(8,128)(2,1)S(1)} %collective-permute-done.7, bf16[1328,128]{1,0:T(8,128)(2,1)S(1)} %fusion), dimensions={0} | concatenate | bytes 687104
  83.8 0.1 constant_dynamic-slice_fusion
  83.9 0.1 constant_dynamic-slice_fusion.1
  84.0 0.6 collective-permute-start.6
  84.6 0.9 copy.21
  85.5 6.1 %collective-permute-done.6.other_ref = bf16[656,128]{1,0:T(8,128)(2,1)S(1)} collective-permute-done((bf16[656,128]{1,0:T(8,128)(2,1)S(1)}, bf16[656,128]{1,0:T(8,128)(2,1)S(1)}, u32[]{:S(2)}, u32[]{:S(2)}) %collective-permute-start.6) | collective-permute-done | bytes 167968 | tf_op jit(solution)/shard_map/ppermute | solution.py:277
  91.6 0.9 shard_map.93
  (2 shorter events, 0.0 us)
Async XLA Ops:
  1.7 10.5 %collective-permute-start.2 = (bf16[576,512]{1,0:T(8,128)(2,1)S(1)}, bf16[576,512]{1,0:T(8,128)(2,1)S(1)}, u32[]{:S(2)}, u32[]{:S(2)}) collective-permute-start(bf16[576,512]{1,0:T(8,128)(2,1)S(1)} %slice.9), channel_id=1, source_target_pairs={{0,16},{16,32},{32,48},{48,64},{64,80},{80,96},{96,112},{112,128},... | collective-permute-start | bytes 1769480 | tf_op jit(solution)/shard_map/ppermute | solution.py:202
  6.8 10.6 %collective-permute-start.3 = (bf16[576,512]{1,0:T(8,128)(2,1)S(1)}, bf16[576,512]{1,0:T(8,128)(2,1)S(1)}, u32[]{:S(2)}, u32[]{:S(2)}) collective-permute-start(bf16[576,512]{1,0:T(8,128)(2,1)S(1)} %get-tuple-element.52), channel_id=1, source_target_pairs={{0,16},{16,32},{32,48},{48,64},{64,80},{80,96},{96,112},{112,128},... | collective-permute-start | bytes 1769480 | tf_op jit(solution)/shard_map/ppermute | solution.py:202
  10.1 13.0 %collective-permute-start = (bf16[576,256]{1,0:T(8,128)(2,1)S(1)}, bf16[576,256]{1,0:T(8,128)(2,1)S(1)}, u32[]{:S(2)}, u32[]{:S(2)}) collective-permute-start(bf16[576,256]{1,0:T(8,128)(2,1)S(1)} %get-tuple-element.49.next_ref), channel_id=1, source_target_pairs={{0,16},{16,32},{32,48},{48,64},{64,80},{80,96},{96,112},{112,128},... | collective-permute-start | bytes 884744 | tf_op jit(solution)/shard_map/ppermute | solution.py:202
  11.2 12.5 %collective-permute-start.1 = (bf16[576,256]{1,0:T(8,128)(2,1)S(1)}, bf16[576,256]{1,0:T(8,128)(2,1)S(1)}, u32[]{:S(2)}, u32[]{:S(2)}) collective-permute-start(bf16[576,256]{1,0:T(8,128)(2,1)S(1)} %slice.8), channel_id=1, source_target_pairs={{0,16},{16,32},{32,48},{48,64},{64,80},{80,96},{96,112},{112,128},... | collective-permute-start | bytes 884744 | tf_op jit(solution)/shard_map/ppermute | solution.py:202
  21.3 7.7 %collective-permute-start.5 = (bf16[576,512]{1,0:T(8,128)(2,1)S(1)}, bf16[576,512]{1,0:T(8,128)(2,1)S(1)}, u32[]{:S(2)}, u32[]{:S(2)}) collective-permute-start(bf16[576,512]{1,0:T(8,128)(2,1)S(1)} %get-tuple-element.63), channel_id=1, source_target_pairs={{0,240},{16,0},{32,16},{48,32},{64,48},{80,64},{96,80},{112,96},{1... | collective-permute-start | bytes 1769480 | tf_op jit(solution)/shard_map/ppermute | solution.py:202
  26.7 6.5 %collective-permute-start.4 = (bf16[576,256]{1,0:T(8,128)(2,1)S(1)}, bf16[576,256]{1,0:T(8,128)(2,1)S(1)}, u32[]{:S(2)}, u32[]{:S(2)}) collective-permute-start(bf16[576,256]{1,0:T(8,128)(2,1)S(1)} %get-tuple-element.58), channel_id=1, source_target_pairs={{0,240},{16,0},{32,16},{48,32},{64,48},{80,64},{96,80},{112,96},{1... | collective-permute-start | bytes 884744 | tf_op jit(solution)/shard_map/ppermute | solution.py:202
  37.3 44.0 %copy-start = (u32[256]{0:T(256)S(1)}, u32[256]{0:T(256)}, u32[]{:S(2)}) copy-start(u32[256]{0:T(256)} %constant.43) | copy-start | bytes 3076
  78.0 4.5 %collective-permute-start.7 = (bf16[14,128]{1,0:T(8,128)(2,1)S(1)}, bf16[14,128]{1,0:T(8,128)(2,1)S(1)}, u32[]{:S(2)}, u32[]{:S(2)}) collective-permute-start(bf16[14,128]{1,0:T(8,128)(2,1)S(1)} %slice.10), channel_id=1, source_target_pairs={{0,1},{1,2},{2,3},{3,4},{4,5},{5,6},{6,7},{8,9},{9,10},{10,11},{11... | collective-permute-start | bytes 10760
  84.0 7.6 %collective-permute-start.6 = (bf16[656,128]{1,0:T(8,128)(2,1)S(1)}, bf16[656,128]{1,0:T(8,128)(2,1)S(1)}, u32[]{:S(2)}, u32[]{:S(2)}) collective-permute-start(bf16[656,128]{1,0:T(8,128)(2,1)S(1)} %get-tuple-element.86), channel_id=1, source_target_pairs={{0,8},{1,9},{2,10},{3,11},{4,12},{5,13},{6,14},{7,15},{8,0},{9,1},... | collective-permute-start | bytes 503816 | tf_op jit(solution)/shard_map/ppermute | solution.py:277
